TPU v7x, 32 devices: a whole 2x2x4 slice. The times are simulated.
32 devices in a mesh: seq: 4 (over y, core), batch: 8 (over z, x).
Axes of the slice: x: 2, y: 2, z: 4, core: 2. Of those that a mesh axis runs over, the one named last changes fastest.
Arguments:
- tokens: bfloat16 [24, 1024, 768], P('batch', 'seq'), may hold values from -6 to 6
- cotangent: bfloat16 [24, 1024, 768], P('batch', 'seq'), may hold values from -6 to 6
- lengths: int32 [24], P('batch'), may hold values from 512 to 1024, as said below
- norm1_gain: float32 [768], replicated, may hold values from 0.1 to 1.9
- norm1_shift: float32 [768], replicated, may hold values from -3 to 3
- in_weight: bfloat16 [768, 2304], replicated, may hold values from -0.21875 to 0.21875
- in_bias: float32 [2304], replicated, may hold values from -3 to 3
- conv_weight: float32 [3, 2304], replicated, may hold values from -3.5 to 3.5
- conv_bias: float32 [2304], replicated, may hold values from -3 to 3
- filter_in: float32 [33, 64], replicated, may hold values from -1 to 1
- filter_in_bias: float32 [64], replicated, may hold values from -4 to 4
- filter_mid: float32 [64, 64], replicated, may hold values from -0.75 to 0.75
- filter_mid_bias: float32 [64], replicated, may hold values from -4 to 4
- filter_last: float32 [64, 64], replicated, may hold values from -0.75 to 0.75
- filter_last_bias: float32 [64], replicated, may hold values from -4 to 4
- filter_out: float32 [64, 768], replicated, may hold values from -0.046875 to 0.046875
- decay_rate: float32 [768], replicated, may hold values from 0.3 to 30
- skip_gain: float32 [768], replicated, may hold values from -4 to 4
- out_weight: bfloat16 [768, 768], replicated, may hold values from -0.21875 to 0.21875
- out_bias: float32 [768], replicated, may hold values from -2 to 2
- norm2_gain: float32 [768], replicated, may hold values from 0.1 to 1.9
- norm2_shift: float32 [768], replicated, may hold values from -3 to 3
- up_weight: bfloat16 [768, 3072], replicated, may hold values from -0.21875 to 0.21875
- up_bias: float32 [3072], replicated, may hold values from -3 to 3
- down_weight: bfloat16 [3072, 768], replicated, may hold values from -0.109375 to 0.109375
- down_bias: float32 [768], replicated, may hold values from -2 to 2
Outputs:
- block_out: bfloat16 [24, 1024, 768], P('batch', 'seq')
- grad_tokens: float32 [24, 1024, 768], P('batch', 'seq')
- grad_norm1_gain: float32 [768], replicated
- grad_norm1_shift: float32 [768], replicated
- grad_in_weight: float32 [768, 2304], replicated
- grad_in_bias: float32 [2304], replicated
- grad_conv_weight: float32 [3, 2304], replicated
- grad_conv_bias: float32 [2304], replicated
- grad_filter_in: float32 [33, 64], replicated
- grad_filter_in_bias: float32 [64], replicated
- grad_filter_mid: float32 [64, 64], replicated
- grad_filter_mid_bias: float32 [64], replicated
- grad_filter_last: float32 [64, 64], replicated
- grad_filter_last_bias: float32 [64], replicated
- grad_filter_out: float32 [64, 768], replicated
- grad_decay_rate: float32 [768], replicated
- grad_skip_gain: float32 [768], replicated
- grad_out_weight: float32 [768, 768], replicated
- grad_out_bias: float32 [768], replicated
- grad_norm2_gain: float32 [768], replicated
- grad_norm2_shift: float32 [768], replicated
- grad_up_weight: float32 [768, 3072], replicated
- grad_up_bias: float32 [3072], replicated
- grad_down_weight: float32 [3072, 768], replicated
- grad_down_bias: float32 [768], replicated
Inputs may be any that keep to these rules, and one draw needn't show every extreme that they name: `lengths`: on each index of batch, one of its 3 buckets, chosen by the seed, has length 1024.
All inputs are finite; a program needn't handle non-finite values.
Results may differ from a plain program's by a relative error of at most 0.011.
Values may be sent and summed in bfloat16 or wider, within the bound.
No kernel may reach another device: no remote copies, remote signals or barrier semaphores. Data moves between devices by JAX's collectives and lax.ppermute only.
A program may use at most 320 MiB of HBM per device.

v0:
```python
from functools import partial
import math

import jax
import jax.numpy as jnp
from jax import lax
from jax.sharding import PartitionSpec as P

norm_eps = 1e-05
window_floor = 0.05
highest = lax.Precision.HIGHEST


def shifted(array, axis, by):
    count = lax.axis_size(axis)
    pairs = [(i, i + by) for i in range(count) if 0 <= i + by < count]
    return lax.ppermute(array, axis, pairs)


def layer_norm(values, scales, offset):
    center = values - jnp.mean(values, axis=-1, keepdims=True)
    spread = jnp.mean(center * center, axis=-1, keepdims=True)
    return center * lax.rsqrt(spread + norm_eps) * scales + offset


def features(seq_total, emb_width):
    band_count = (emb_width - 1) // 2
    steps_int = jnp.arange(seq_total, dtype=jnp.int32)
    harmonic = jnp.arange(1, band_count + 1, dtype=jnp.int32)
    phases = steps_int[:, None] * harmonic[None, :] % seq_total
    angles = phases.astype(jnp.float32) * (2.0 * math.pi / seq_total)
    time_ramp = steps_int.astype(jnp.float32) / seq_total
    table = jnp.concatenate([time_ramp[:, None], jnp.cos(angles), jnp.sin(angles)], axis=1)
    return (table, time_ramp)


def filter_taps(
    seq_total,
    filter_in,
    filter_in_bias,
    filter_mid,
    filter_mid_bias,
    filter_last,
    filter_last_bias,
    filter_out,
    decay_rate,
):
    table, time_ramp = features(seq_total, filter_in.shape[0])
    hidden = jnp.sin(jnp.dot(table, filter_in, precision=highest) + filter_in_bias)
    hidden = jnp.sin(jnp.dot(hidden, filter_mid, precision=highest) + filter_mid_bias)
    hidden = jnp.sin(jnp.dot(hidden, filter_last, precision=highest) + filter_last_bias)
    shaped = jnp.dot(hidden, filter_out, precision=highest)
    window = jnp.exp(-time_ramp[:, None] * decay_rate[None, :]) + window_floor
    return shaped * window


def short_conv(extended, conv_weight, conv_bias):
    return (
        conv_weight[0] * extended[:, :-2]
        + conv_weight[1] * extended[:, 1:-1]
        + conv_weight[2] * extended[:, 2:]
        + conv_bias
    )


def dft_tables(span_len, length_in):
    freqs = jnp.arange(span_len // 2 + 1, dtype=jnp.int32)
    places = jnp.arange(length_in, dtype=jnp.int32)
    phases = freqs[:, None] * places[None, :] % span_len
    angles = phases.astype(jnp.float32) * (2.0 * math.pi / span_len)
    return (jnp.cos(angles), jnp.sin(angles))


def inverse_tables(span_len, first_row, row_count):
    places = first_row + jnp.arange(row_count, dtype=jnp.int32)
    freqs = jnp.arange(span_len // 2 + 1, dtype=jnp.int32)
    phases = places[:, None] * freqs[None, :] % span_len
    angles = phases.astype(jnp.float32) * (2.0 * math.pi / span_len)
    weights = jnp.where((freqs == 0) | (2 * freqs == span_len), 1.0, 2.0) / span_len
    return (jnp.cos(angles) * weights[None, :], jnp.sin(angles) * weights[None, :])


def rows_spectrum(values, span_len):
    cos_table, sin_table = dft_tables(span_len, values.shape[1])
    real_part = jnp.einsum("ft,btk->bfk", cos_table, values, precision=highest)
    imag_part = -jnp.einsum("ft,btk->bfk", sin_table, values, precision=highest)
    return (real_part, imag_part)


def window_spectrum(window, span_len):
    cos_table, sin_table = dft_tables(span_len, window.shape[0])
    real_part = jnp.einsum("ft,tk->fk", cos_table, window, precision=highest)
    imag_part = -jnp.einsum("ft,tk->fk", sin_table, window, precision=highest)
    return (real_part, imag_part)


def rows_back(real_part, imag_part, span_len, first_row, row_count):
    inv_cos, inv_sin = inverse_tables(span_len, first_row, row_count)
    return jnp.einsum("tf,bfk->btk", inv_cos, real_part, precision=highest) - jnp.einsum(
        "tf,bfk->btk", inv_sin, imag_part, precision=highest
    )


def apply_window(piece_real, piece_imag, win_real, win_imag):
    out_real = piece_real * win_real[None] - piece_imag * win_imag[None]
    out_imag = piece_real * win_imag[None] + piece_imag * win_real[None]
    return (out_real, out_imag)


def causal_terms(taps_pad, incoming, own_start, own_rows, seq_total):
    piece_rows = incoming.shape[1]
    span_len = piece_rows + own_rows
    slice_at = own_start - piece_rows + 1 + seq_total
    window = lax.dynamic_slice_in_dim(taps_pad, slice_at, span_len - 1, 0)
    piece_real, piece_imag = rows_spectrum(incoming.astype(jnp.float32), span_len)
    win_real, win_imag = window_spectrum(window, span_len)
    out_real, out_imag = apply_window(piece_real, piece_imag, win_real, win_imag)
    return rows_back(out_real, out_imag, span_len, piece_rows - 1, own_rows)


def reverse_terms(taps_pad, incoming, begin_row, own_start, own_product, seq_total):
    piece_rows = incoming.shape[1]
    own_rows = own_product.shape[1]
    span_len = piece_rows + own_rows
    slice_at = begin_row - own_start - own_rows + 1 + seq_total
    window = jnp.flip(lax.dynamic_slice_in_dim(taps_pad, slice_at, span_len - 1, 0), axis=0)
    grad_real, grad_imag = rows_spectrum(incoming.astype(jnp.float32), span_len)
    win_real, win_imag = window_spectrum(window, span_len)
    out_real, out_imag = apply_window(grad_real, grad_imag, win_real, win_imag)
    back_part = rows_back(out_real, out_imag, span_len, piece_rows - 1, own_rows)
    flipped = jnp.flip(own_product.astype(jnp.float32), axis=1)
    prod_real, prod_imag = rows_spectrum(flipped, span_len)
    lag_real = jnp.sum(grad_real * prod_real - grad_imag * prod_imag, axis=0)
    lag_imag = jnp.sum(grad_real * prod_imag + grad_imag * prod_real, axis=0)
    lag_part = rows_back(lag_real[None], lag_imag[None], span_len, 0, span_len - 1)[0]
    return (back_part, lag_part, slice_at)


def shards(
    tokens,
    cotangent,
    lengths,
    norm1_gain,
    norm1_shift,
    in_weight,
    in_bias,
    conv_weight,
    conv_bias,
    filter_in,
    filter_in_bias,
    filter_mid,
    filter_mid_bias,
    filter_last,
    filter_last_bias,
    filter_out,
    decay_rate,
    skip_gain,
    out_weight,
    out_bias,
    norm2_gain,
    norm2_shift,
    up_weight,
    up_bias,
    down_weight,
    down_bias,
):
    block_count, own_rows, width = tokens.shape
    seq_total = own_rows * lax.axis_size("seq")
    own_start = lax.axis_index("seq") * own_rows
    positions = own_start + jnp.arange(own_rows, dtype=jnp.int32)
    mask = (positions[None, :] < lengths[:, None]).astype(jnp.float32)[:, :, None]
    tokens_f = tokens.astype(jnp.float32)
    normed_f, norm1_pull = jax.vjp(layer_norm, tokens_f, norm1_gain, norm1_shift)
    normed = normed_f.astype(jnp.bfloat16)
    mixed_in = (
        jnp.einsum("bnd,de->bne", normed, in_weight, preferred_element_type=jnp.float32) + in_bias
    ).astype(jnp.bfloat16)
    borrowed = shifted(mixed_in[:, own_rows - 2 :, :], "seq", 1)
    extended = jnp.concatenate([borrowed, mixed_in], axis=1).astype(jnp.float32)
    shorted, short_pull = jax.vjp(short_conv, extended, conv_weight, conv_bias)
    gate_out = shorted[:, :, :width]
    gate_in = shorted[:, :, width : 2 * width]
    values = shorted[:, :, 2 * width :]
    product = (values * gate_in * mask).astype(jnp.bfloat16)
    product_f = product.astype(jnp.float32)
    taps, taps_pull = jax.vjp(
        partial(filter_taps, seq_total),
        filter_in,
        filter_in_bias,
        filter_mid,
        filter_mid_bias,
        filter_last,
        filter_last_bias,
        filter_out,
        decay_rate,
    )
    taps_pad = jnp.concatenate([jnp.zeros((seq_total, width), jnp.float32), taps], axis=0)
    incoming = lax.all_gather(product, "seq", axis=1, tiled=True)
    result = causal_terms(taps_pad, incoming, own_start, own_rows, seq_total)
    convolved = result
    gated = ((convolved + skip_gain * product_f) * gate_out).astype(jnp.bfloat16)
    mixer = (
        jnp.einsum("bnd,de->bne", gated, out_weight, preferred_element_type=jnp.float32) + out_bias
    )
    resid = tokens_f + mask * mixer
    normed2_f, norm2_pull = jax.vjp(layer_norm, resid, norm2_gain, norm2_shift)
    normed2 = normed2_f.astype(jnp.bfloat16)
    upward = (
        jnp.einsum("bnd,df->bnf", normed2, up_weight, preferred_element_type=jnp.float32) + up_bias
    )
    active_f, gelu_pull = jax.vjp(partial(jax.nn.gelu, approximate=False), upward)
    active = active_f.astype(jnp.bfloat16)
    downward = (
        jnp.einsum("bnf,fd->bnd", active, down_weight, preferred_element_type=jnp.float32)
        + down_bias
    )
    block_out = (resid + mask * downward).astype(jnp.bfloat16)
    cot_f = cotangent.astype(jnp.float32)
    d_down = (mask * cot_f).astype(jnp.bfloat16)
    grad_down_weight = jnp.einsum("bnf,bnd->fd", active, d_down, preferred_element_type=jnp.float32)
    grad_down_bias = jnp.sum(d_down.astype(jnp.float32), axis=(0, 1))
    d_active = jnp.einsum("bnd,fd->bnf", d_down, down_weight, preferred_element_type=jnp.float32)
    d_upward = gelu_pull(d_active)[0].astype(jnp.bfloat16)
    grad_up_weight = jnp.einsum(
        "bnd,bnf->df", normed2, d_upward, preferred_element_type=jnp.float32
    )
    grad_up_bias = jnp.sum(d_upward.astype(jnp.float32), axis=(0, 1))
    d_normed2 = jnp.einsum("bnf,df->bnd", d_upward, up_weight, preferred_element_type=jnp.float32)
    d_resid_norm, grad_norm2_gain, grad_norm2_shift = norm2_pull(d_normed2)
    d_resid = cot_f + d_resid_norm
    d_mixer = (mask * d_resid).astype(jnp.bfloat16)
    grad_out_weight = jnp.einsum("bnd,bne->de", gated, d_mixer, preferred_element_type=jnp.float32)
    grad_out_bias = jnp.sum(d_mixer.astype(jnp.float32), axis=(0, 1))
    d_gated = jnp.einsum("bne,de->bnd", d_mixer, out_weight, preferred_element_type=jnp.float32)
    d_convolved = (d_gated * gate_out).astype(jnp.bfloat16)
    grad_skip_gain = jnp.sum(d_gated * gate_out * product_f, axis=(0, 1))
    incoming = lax.all_gather(d_convolved, "seq", axis=1, tiled=True)
    begin_row = jnp.int32(0)
    taps_ext = jnp.zeros((2 * seq_total, width), jnp.float32)
    back_part, lag_part, slice_at = reverse_terms(
        taps_pad, incoming, begin_row, own_start, product, seq_total
    )
    result = (back_part, lax.dynamic_update_slice_in_dim(taps_ext, lag_part, slice_at, 0))
    back_conv, taps_ext = result
    d_taps = taps_ext[seq_total:]
    d_product = back_conv + d_gated * gate_out * skip_gain
    d_short = jnp.concatenate(
        [
            d_gated * (convolved + skip_gain * product_f),
            d_product * values * mask,
            d_product * gate_in * mask,
        ],
        axis=2,
    )
    d_extended, grad_conv_weight, grad_conv_bias = short_pull(d_short)
    arriving = shifted(d_extended[:, :2, :].astype(jnp.bfloat16), "seq", -1).astype(jnp.float32)
    d_mixed = d_extended[:, 2:, :].at[:, own_rows - 2 :, :].add(arriving)
    g_mixed = d_mixed.astype(jnp.bfloat16)
    grad_in_weight = jnp.einsum("bnd,bne->de", normed, g_mixed, preferred_element_type=jnp.float32)
    grad_in_bias = jnp.sum(g_mixed.astype(jnp.float32), axis=(0, 1))
    d_normed = jnp.einsum("bne,de->bnd", g_mixed, in_weight, preferred_element_type=jnp.float32)
    d_tokens_norm, grad_norm1_gain, grad_norm1_shift = norm1_pull(d_normed)
    grad_tokens = d_resid + d_tokens_norm
    (
        grad_filter_in,
        grad_filter_in_bias,
        grad_filter_mid,
        grad_filter_mid_bias,
        grad_filter_last,
        grad_filter_last_bias,
        grad_filter_out,
        grad_decay_rate,
    ) = taps_pull(d_taps)
    (
        grad_norm1_gain,
        grad_norm1_shift,
        grad_in_weight,
        grad_in_bias,
        grad_conv_weight,
        grad_conv_bias,
        grad_filter_in,
        grad_filter_in_bias,
        grad_filter_mid,
        grad_filter_mid_bias,
        grad_filter_last,
        grad_filter_last_bias,
        grad_filter_out,
        grad_decay_rate,
        grad_skip_gain,
        grad_out_weight,
        grad_out_bias,
        grad_norm2_gain,
        grad_norm2_shift,
        grad_up_weight,
        grad_up_bias,
        grad_down_weight,
        grad_down_bias,
    ) = lax.psum(
        (
            grad_norm1_gain,
            grad_norm1_shift,
            grad_in_weight,
            grad_in_bias,
            grad_conv_weight,
            grad_conv_bias,
            grad_filter_in,
            grad_filter_in_bias,
            grad_filter_mid,
            grad_filter_mid_bias,
            grad_filter_last,
            grad_filter_last_bias,
            grad_filter_out,
            grad_decay_rate,
            grad_skip_gain,
            grad_out_weight,
            grad_out_bias,
            grad_norm2_gain,
            grad_norm2_shift,
            grad_up_weight,
            grad_up_bias,
            grad_down_weight,
            grad_down_bias,
        ),
        ("seq", "batch"),
    )
    return (
        block_out,
        grad_tokens,
        grad_norm1_gain,
        grad_norm1_shift,
        grad_in_weight,
        grad_in_bias,
        grad_conv_weight,
        grad_conv_bias,
        grad_filter_in,
        grad_filter_in_bias,
        grad_filter_mid,
        grad_filter_mid_bias,
        grad_filter_last,
        grad_filter_last_bias,
        grad_filter_out,
        grad_decay_rate,
        grad_skip_gain,
        grad_out_weight,
        grad_out_bias,
        grad_norm2_gain,
        grad_norm2_shift,
        grad_up_weight,
        grad_up_bias,
        grad_down_weight,
        grad_down_bias,
    )


def solution(mesh):
    placed = (
        P("batch", "seq", None),
        P("batch", "seq", None),
        P("batch"),
        P(),
        P(),
        P(),
        P(),
        P(),
        P(),
        P(),
        P(),
        P(),
        P(),
        P(),
        P(),
        P(),
        P(),
        P(),
        P(),
        P(),
        P(),
        P(),
        P(),
        P(),
        P(),
        P(),
    )
    return jax.shard_map(
        shards,
        mesh=mesh,
        in_specs=placed,
        out_specs=(
            P("batch", "seq", None),
            P("batch", "seq", None),
            P(),
            P(),
            P(),
            P(),
            P(),
            P(),
            P(),
            P(),
            P(),
            P(),
            P(),
            P(),
            P(),
            P(),
            P(),
            P(),
            P(),
            P(),
            P(),
            P(),
            P(),
            P(),
            P(),
        ),
        check_vma=False,
    )
```

profile of v0, /device:TPU:0, one launch (start us, length us, event | category | flops | bytes accessed | tf_op | source)
XLA Modules:
  0.0 1231.1 jit_solution(2835407891307420063)
XLA Ops:
  7.3 1.6 convert_reduce_fusion.2
  8.9 1.7 fusion.105
  11.3 5.3 add_convert_fusion.1
  16.6 1.8 copy-done.33
  19.1 3.0 collective-permute-start
  23.1 2.7 maximum_convert_fusion
  25.9 2.3 add_add_fusion
  28.8 3.0 copy-done.4
  33.7 2.7 fusion.297
  36.5 2.7 fusion.298
  39.2 2.7 fusion.299
  41.9 5.8 fusion.71
  47.7 22.7 %fusion.55 = f32[641,768]{1,0:T(8,128)} fusion(s32[]{:T(128)S(6)} %select_n.97, f32[1024,768]{1,0:T(8,128)S(1)} %get-tuple-element.101), kind=kOutput, calls=%fused_computation.102 | convolution fusion | flops 7563014656 | bytes 5114884 | tf_op jit(solution)/shard_map/ft,tk->fk/dot_general | solution.py:92
  70.4 22.9 %fusion.148 = f32[641,768]{1,0:T(8,128)} fusion(s32[]{:T(128)S(6)} %select_n.97, f32[1024,768]{1,0:T(8,128)S(1)} %get-tuple-element.101), kind=kOutput, calls=%fused_computation.195 | convolution fusion | flops 7563507200 | bytes 5114884 | tf_op jit(solution)/shard_map/ft,tk->fk/dot_general | solution.py:93
  93.3 24.0 %fusion.90 = f32[3,768,641]{1,2,0:T(8,128)S(1)} fusion(bf16[3,1024,768]{2,1,0:T(8,128)(2,1)} %all-gather.3.cloned.1.call-done), kind=kOutput, calls=%fused_computation.138 | convolution fusion | flops 18153611264 | bytes 10626048 | tf_op jit(solution)/shard_map/ft,btk->bfk/dot_general | solution.py:85
  117.2 21.3 %fusion.86 = f32[3,768,641]{1,2,0:T(8,128)S(1)} fusion(bf16[3,1024,768]{2,1,0:T(8,128)(2,1)S(1)} %copy-done.109), kind=kOutput, calls=%fused_computation.134 | convolution fusion | flops 18153611264 | bytes 10626048 | tf_op jit(solution)/shard_map/ft,btk->bfk/dot_general | solution.py:86
  138.6 2.6 copy-done.11
  141.2 13.6 %fusion.16 = f32[3,768,256]{1,2,0:T(8,128)} fusion(f32[3,768,641]{1,2,0:T(8,128)S(1)} %fusion.90, f32[3,768,641]{1,2,0:T(8,128)S(1)} %fusion.86, f32[641,768]{1,0:T(8,128)} %fusion.148, f32[641,768]{1,0:T(8,128)} %fusion.55, f32[641]{0:T(1024)S(1)} %select_multiply_fusion, s32[256]{0:T(256)S(1)} %iota_add_fusion), kind=kOutput, calls=%fused_computation.50 | convolution fusion | flops 4544474624 | bytes 18116100 | tf_op jit(solution)/shard_map/tf,bfk->btk/dot_general | solution.py:99
  154.8 16.6 %multiply_convert_fusion.2 = (bf16[3,256,768]{2,1,0:T(8,128)(2,1)S(1)}, f32[3,256,768]{2,1,0:T(8,128)}) fusion(f32[3,256,2304]{2,1,0:T(8,128)S(1)} %bitcast.201, bf16[3,256,768]{2,1,0:T(8,128)(2,1)S(1)} %copy-done.9, f32[768]{0:T(1024)S(1)} %copy-done.95, f32[3,768,256]{1,2,0:T(8,128)} %fusion.16, f32[641]{0:T(1024)S(1)} %select_multiply_fusion, ...), kind=kOutput, calls=%fused_computation.166 | convolution fusion | flops 4548013568 | bytes 25197060 | tf_op jit(solution)/shard_map/tf,bfk->btk/dot_general | solution.py:99
  171.5 3.0 fusion.300
  175.0 9.3 fusion.108
  184.3 23.3 %multiply_convert_fusion = (bf16[3,256,3072]{2,1,0:T(8,128)(2,1)}, f32[3,256,3072]{2,1,0:T(8,128)}) fusion(f32[3,256,3072]{2,1,0:T(8,128)S(1)} %get-tuple-element.107, f32[3072]{0:T(1024)S(1)} %copy-done.98, u8[256,3072]{1,0:T(8,128)(4,1)S(1)} %get-tuple-element.43, u8[256,3072]{1,0:T(8,128)(4,1)S(1)} %get-tuple-element.42), kind=kLoop, calls=%fused_computation.9 | loop fusion | flops 167510016 | bytes 25178112 | tf_op jit(solution)/shard_map/convert_element_type | solution.py:212
  207.6 13.9 %convert_reduce_fusion = (f32[3072]{0:T(1024)}, bf16[3,256,3072]{2,1,0:T(8,128)(2,1)}) fusion(f32[3,256,3072]{2,1,0:T(8,128)} %get-tuple-element.83, bf16[3072,768]{1,0:T(8,128)(2,1)} %param.52, bf16[3,256,768]{2,1,0:T(8,128)(2,1)} %param.29, f32[3,256]{1,0:T(4,128)S(1)} %copy-done.70, f32[3,256,3072]{2,1,0:T(8,128)} %copy-done.22, f32[3072]{0:T(1024)S(1)} %copy-done.98), kind=kOutput, calls=%fused_computation.7 | convolution fusion | flops 3665753088 | bytes 29518848 | tf_op jit(solution)/shard_map/bnd,fd->bnf/dot_general | solution.py:222
  221.6 9.4 multiply_reduce_fusion.4
  235.6 4.4 multiply_reduce_fusion.5
  240.1 4.5 pad_dynamic-slice_fusion
  244.6 31.7 %rev.8 = f32[1279,768]{1,0:T(8,128)} reverse(f32[1279,768]{1,0:T(8,128)} %pad_dynamic-slice_fusion), dimensions={0} | reverse | bytes 7858176 | tf_op jit(solution)/shard_map/jit(_flip)/rev | solution.py:126
  276.2 24.2 %fusion.62 = f32[641,768]{1,0:T(8,128)} fusion(f32[1279,768]{1,0:T(8,128)} %rev.8), kind=kOutput, calls=%fused_computation.110 | convolution fusion | flops 7563014656 | bytes 5898240 | tf_op jit(solution)/shard_map/ft,tk->fk/dot_general | solution.py:92
  300.5 22.5 %fusion.145 = f32[641,768]{1,0:T(8,128)} fusion(f32[1279,768]{1,0:T(8,128)S(1)} %copy-done.32), kind=kOutput, calls=%fused_computation.194 | convolution fusion | flops 7563507200 | bytes 5898240 | tf_op jit(solution)/shard_map/ft,tk->fk/dot_general | solution.py:93
  323.0 17.8 %rev.9 = f32[3,256,768]{2,1,0:T(8,128)} reverse(bf16[3,256,768]{2,1,0:T(8,128)(2,1)} %multiply_convert_fusion.3), dimensions={1} | reverse | bytes 3538944 | tf_op jit(solution)/shard_map/jit(_flip)/rev | solution.py:131
  340.7 11.5 fusion.176
  352.2 2.5 convolution_bitcast_fusion.3
  354.8 9.0 convolution_bitcast_fusion.1
  363.8 7.4 convolution_bitcast_fusion.2
  371.3 22.4 %fusion.88 = f32[3,768,641]{1,2,0:T(8,128)S(1)} fusion(bf16[3,1024,768]{2,1,0:T(8,128)(2,1)} %all-gather.5.cloned.1.call-done), kind=kOutput, calls=%fused_computation.136 | convolution fusion | flops 18153611264 | bytes 10626048 | tf_op jit(solution)/shard_map/ft,btk->bfk/dot_general | solution.py:85
  393.8 22.3 %fusion.84 = f32[3,768,641]{1,2,0:T(8,128)S(1)} fusion(bf16[3,1024,768]{2,1,0:T(8,128)(2,1)S(1)} %copy-done.110), kind=kOutput, calls=%fused_computation.132 | convolution fusion | flops 18153611264 | bytes 10626048 | tf_op jit(solution)/shard_map/ft,btk->bfk/dot_general | solution.py:86
  416.2 11.5 fusion.10
  427.7 21.2 %multiply_multiply_fusion.6 = (f32[3,256,768]{2,1,0:T(8,128)}, f32[3,256,768]{2,1,0:T(8,128)}) fusion(f32[3,256,2304]{2,1,0:T(8,128)} %copy-done.4, f32[3,256]{1,0:T(4,128)S(1)} %copy-done.72, f32[768]{0:T(1024)S(1)} %copy-done.96, f32[3,256,768]{2,1,0:T(8,128)} %get-tuple-element.109, f32[3,768,256]{1,2,0:T(8,128)} %fusion.10, f32[641]{0:T(1024)S(1)} %copy-done.68, ...), kind=kOutput, calls=%fused_computation.160 | convolution fusion | flops 4549193216 | bytes 32278020 | tf_op jit(solution)/shard_map/tf,bfk->btk/dot_general | solution.py:99
  448.9 10.1 multiply_reduce_fusion.2
  459.0 11.2 pad_add_fusion
  470.2 2.4 slice.121
  472.7 1.5 collective-permute-start.1
  475.5 10.7 fusion.8
  486.2 25.7 %fusion.34 = f32[768,1279]{0,1:T(8,128)S(1)} fusion(f32[641,768]{1,0:T(8,128)S(1)} %get-tuple-element.38, f32[641]{0:T(1024)S(1)} %copy-done.68), kind=kOutput, calls=%fused_computation.75 | convolution fusion | flops 7563834368 | bytes 5900804 | tf_op jit(solution)/shard_map/tf,bfk->btk/dot_general | solution.py:99
  511.9 26.6 %subtract_bitcast_fusion = f32[1279,768]{1,0:T(8,128)} fusion(f32[768,1279]{0,1:T(8,128)S(1)} %fusion.34, f32[641,768]{1,0:T(8,128)S(1)} %get-tuple-element.37, f32[641]{0:T(1024)S(1)} %copy-done.68), kind=kOutput, calls=%fused_computation.74 | convolution fusion | flops 7564816896 | bytes 9829892 | tf_op jit(solution)/shard_map/tf,bfk->btk/dot_general | solution.py:99
  538.5 3.1 broadcast_in_dim.37
  541.6 10.6 dynamic_update_slice.3
  552.2 5.3 fusion.109
  557.5 6.7 fusion.303
  565.2 1.9 fusion.302
  568.0 1.9 fusion.301
  569.9 1.4 multiply_reduce_fusion.3
  572.9 3.8 slice.86
  577.7 3.6 fusion.294
  582.8 1.8 fusion.103
  584.7 8.5 convolution_bitcast_fusion
  593.9 9.5 add_convert_fusion.2
  603.4 2.1 add_add_fusion.3
  605.6 137.4 %all-reduce.12.cloned.1.call-done = (f32[768]{0:T(1024)}, f32[768]{0:T(1024)}, f32[2304]{0:T(1024)}, f32[3,2304]{1,0:T(4,128)}, f32[2304]{0:T(1024)}, /*index=5*...) async-done(((f32[768]{0:T(1024)}, f32[768]{0:T(1024)}, ...) | async-done | bytes 124944 | tf_op jit(solution)/shard_map/psum | solution.py:298
  742.9 448.0 %all-reduce.14.cloned.1.call-done = (f32[768,2304]{1,0:T(8,128)}, f32[64,768]{1,0:T(8,128)}, f32[768,768]{1,0:T(8,128)}, f32[768,3072]{1,0:T(8,128)}, f32[3072,768]{1,0:T(8,128)}) async-done(((f32[768,2304]{1,0:T(8,128)}, f32[64,768]{1,0:T(8,128)}, f32[768,768]{1,0:T(8,128)}, f32[768,3072]{1,0:T(8,128)}, f32[3072,768]{1,0:T(8,128)}), (f32[768,2304]{1,0:T(8,128)}, f32[64,768]{1,0:T(8,128)}, ...) | async-done | bytes 28508176 | tf_op jit(solution)/shard_map/psum | solution.py:298
  1193.5 6.6 copy.108
  1207.2 1.4 copy.121
  1210.4 8.8 copy.125
  1219.8 3.7 copy.127
  (326 shorter events, 30.7 us)
Async XLA Ops:
  7.2 86.0 %all-gather.3.cloned.1.call-start = ((), (), s32[]{:S(2)}) async-start(), calls=%async_computation | async-start | bytes 5898240 | tf_op jit(solution)/shard_map/all_gather | solution.py:198
  11.3 10.8 copy-start.108
  19.1 4.0 collective-permute-start
  22.1 149.4 %copy-start.69 = (f32[3,256]{1,0:T(4,128)}, f32[3,256]{1,0:T(4,128)S(1)}, u32[]{:S(2)}) copy-start(f32[3,256]{1,0:T(4,128)S(1)} %compare_convert_fusion) | copy-start | bytes 9220
  31.7 10.1 copy-start.93
  33.0 338.2 %all-gather.5.cloned.1.call-start = ((), (), s32[]{:S(2)}) async-start(), calls=%async_computation.1 | async-start | bytes 5898240 | tf_op jit(solution)/shard_map/all_gather | solution.py:237
  33.3 121.4 %copy-start.90 = (s32[256]{0:T(256)}, s32[256]{0:T(256)S(1)}, u32[]{:S(2)}) copy-start(s32[256]{0:T(256)S(1)} %iota_add_fusion) | copy-start | bytes 3076
  33.3 14.4 %copy-start.85 = (f32[1024]{0:T(1024)}, f32[1024]{0:T(1024)S(1)}, u32[]{:S(2)}) copy-start(f32[1024]{0:T(1024)S(1)} %multiply_negate_fusion.1) | copy-start | bytes 12292
  33.4 121.4 %copy-start.67 = (f32[641]{0:T(1024)}, f32[641]{0:T(1024)S(1)}, u32[]{:S(2)}) copy-start(f32[641]{0:T(1024)S(1)} %select_multiply_fusion) | copy-start | bytes 7696
  47.7 22.7 %copy-start.19 = (f32[1024,768]{1,0:T(8,128)}, f32[1024,768]{1,0:T(8,128)S(1)}, u32[]{:S(2)}) copy-start(f32[1024,768]{1,0:T(8,128)S(1)} %get-tuple-element.101) | copy-start | bytes 9437188
  93.2 24.0 %copy-start.109 = (bf16[3,1024,768]{2,1,0:T(8,128)(2,1)S(1)}, bf16[3,1024,768]{2,1,0:T(8,128)(2,1)}, u32[]{:S(2)}) copy-start(bf16[3,1024,768]{2,1,0:T(8,128)(2,1)} %all-gather.3.cloned.1.call-done) | copy-start | bytes 14155780
  93.2 61.5 %slice-start.6 = ((s8[7077888]{0:T(1024)(128)(4,1)}), s8[4194304]{0:T(1024)(128)(4,1)S(1)}, s32[]{:S(2)}) async-start(s8[7077888]{0:T(1024)(128)(4,1)} %bitcast.200), calls=%async_computation.10 | async-start | bytes 8388608
  117.2 37.5 %slice-start.7 = ((s8[7077888]{0:T(1024)(128)(4,1)}), s8[2883584]{0:T(1024)(128)(4,1)S(1)}, s32[]{:S(2)}) async-start(s8[7077888]{0:T(1024)(128)(4,1)} %bitcast.200), calls=%async_computation.11 | async-start | bytes 5767168
  141.2 13.6 %copy-start.9 = (bf16[3,256,768]{2,1,0:T(8,128)(2,1)S(1)}, bf16[3,256,768]{2,1,0:T(8,128)(2,1)}, u32[]{:S(2)}) copy-start(bf16[3,256,768]{2,1,0:T(8,128)(2,1)} %multiply_convert_fusion.3) | copy-start | bytes 3538948
  141.2 13.6 %copy-start.95 = (f32[768]{0:T(1024)S(1)}, f32[768]{0:T(1024)}, u32[]{:S(2)}) copy-start(f32[768]{0:T(1024)} %param.45) | copy-start | bytes 9220
  154.8 16.7 %copy-start.6 = (bf16[3,256,768]{2,1,0:T(8,128)(2,1)S(1)}, bf16[3,256,768]{2,1,0:T(8,128)(2,1)}, u32[]{:S(2)}) copy-start(bf16[3,256,768]{2,1,0:T(8,128)(2,1)} %param.28) | copy-start | bytes 3538948
  154.8 16.7 %copy-start.111 = (f32[768]{0:T(1024)S(1)}, f32[768]{0:T(1024)}, u32[]{:S(2)}) copy-start(f32[768]{0:T(1024)} %param.47) | copy-start | bytes 9220
  174.5 9.8 copy-start.12
  184.3 23.3 %copy-start.22 = (f32[3,256,3072]{2,1,0:T(8,128)}, f32[3,256,3072]{2,1,0:T(8,128)S(1)}, u32[]{:S(2)}) copy-start(f32[3,256,3072]{2,1,0:T(8,128)S(1)} %get-tuple-element.107) | copy-start | bytes 28311556
  184.3 23.3 %copy-start.70 = (f32[3,256]{1,0:T(4,128)S(1)}, f32[3,256]{1,0:T(4,128)}, u32[]{:S(2)}) copy-start(f32[3,256]{1,0:T(4,128)} %copy-done.69) | copy-start | bytes 9220
  240.0 502.9 %all-reduce.12.cloned.1.call-start = ((), (), s32[]{:S(2)}) async-start(), calls=%async_computation.2 | async-start | bytes 388096 | tf_op jit(solution)/shard_map/psum | solution.py:298
  276.2 24.2 %copy-start.32 = (f32[1279,768]{1,0:T(8,128)S(1)}, f32[1279,768]{1,0:T(8,128)}, u32[]{:S(2)}) copy-start(f32[1279,768]{1,0:T(8,128)} %rev.8) | copy-start | bytes 11787268
  340.7 11.5 copy-start.31
  340.7 11.5 copy-start.40
  352.2 11.5 slice-start.13
  371.2 22.5 %copy-start.110 = (bf16[3,1024,768]{2,1,0:T(8,128)(2,1)S(1)}, bf16[3,1024,768]{2,1,0:T(8,128)(2,1)}, u32[]{:S(2)}) copy-start(bf16[3,1024,768]{2,1,0:T(8,128)(2,1)} %all-gather.5.cloned.1.call-done) | copy-start | bytes 14155780
  393.7 22.4 %copy-start.2 = (f32[3,768,641]{1,2,0:T(8,128)}, f32[3,768,641]{1,2,0:T(8,128)S(1)}, u32[]{:S(2)}) copy-start(f32[3,768,641]{1,2,0:T(8,128)S(1)} %fusion.88) | copy-start | bytes 17722372
  393.7 22.4 %copy-start.25 = (f32[641,768]{1,0:T(8,128)S(1)}, f32[641,768]{1,0:T(8,128)}, u32[]{:S(2)}) copy-start(f32[641,768]{1,0:T(8,128)} %fusion.62) | copy-start | bytes 5907460
  393.7 22.4 %copy-start.26 = (f32[641,768]{1,0:T(8,128)S(1)}, f32[641,768]{1,0:T(8,128)}, u32[]{:S(2)}) copy-start(f32[641,768]{1,0:T(8,128)} %fusion.145) | copy-start | bytes 5907460
  393.7 22.4 %copy-start.68 = (f32[641]{0:T(1024)S(1)}, f32[641]{0:T(1024)}, u32[]{:S(2)}) copy-start(f32[641]{0:T(1024)} %copy-done.67) | copy-start | bytes 7696
  393.8 22.4 %copy-start.91 = (s32[256]{0:T(256)S(1)}, s32[256]{0:T(256)}, u32[]{:S(2)}) copy-start(s32[256]{0:T(256)} %copy-done.90) | copy-start | bytes 3076
  416.1 11.5 copy-start.3
  416.1 11.5 copy-start.72
  416.1 11.5 copy-start.96
  427.6 21.2 %slice-start = ((s8[7299072]{0:T(1024)(128)(4,1)}), s8[4194304]{0:T(1024)(128)(4,1)S(1)}, s32[]{:S(2)}) async-start(s8[7299072]{0:T(1024)(128)(4,1)} %bitcast.194), calls=%async_computation.4 | async-start | bytes 8388608
  427.6 21.2 %slice-start.1 = ((s8[7299072]{0:T(1024)(128)(4,1)}), s8[3104768]{0:T(1024)(128)(4,1)S(1)}, s32[]{:S(2)}) async-start(s8[7299072]{0:T(1024)(128)(4,1)} %bitcast.194), calls=%async_computation.5 | async-start | bytes 6209536
  427.7 21.2 %copy-start.62 = (f32[2304]{0:T(1024)S(1)}, f32[2304]{0:T(1024)}, u32[]{:S(2)}) copy-start(f32[2304]{0:T(1024)} %copy-done.61) | copy-start | bytes 27652
  427.7 21.2 %copy-start.64 = (f32[2304]{0:T(1024)S(1)}, f32[2304]{0:T(1024)}, u32[]{:S(2)}) copy-start(f32[2304]{0:T(1024)} %copy-done.63) | copy-start | bytes 27652
  427.7 21.2 %copy-start.66 = (f32[2304]{0:T(1024)S(1)}, f32[2304]{0:T(1024)}, u32[]{:S(2)}) copy-start(f32[2304]{0:T(1024)} %copy-done.65) | copy-start | bytes 27652
  459.0 16.4 %slice-start.2 = ((s8[5971968]{0:T(1024)(128)(4,1)}), s8[4194304]{0:T(1024)(128)(4,1)S(1)}, s32[]{:S(2)}) async-start(s8[5971968]{0:T(1024)(128)(4,1)} %bitcast.196), calls=%async_computation.6 | async-start | bytes 8388608
  459.0 16.4 %slice-start.4 = ((s8[5971968]{0:T(1024)(128)(4,1)}), s8[4194304]{0:T(1024)(128)(4,1)S(1)}, s32[]{:S(2)}) async-start(s8[5971968]{0:T(1024)(128)(4,1)} %bitcast.198), calls=%async_computation.8 | async-start | bytes 8388608
  459.0 16.4 %slice-start.8 = ((s8[5971968]{0:T(1024)(128)(4,1)}), s8[4194304]{0:T(1024)(128)(4,1)S(1)}, s32[]{:S(2)}) async-start(s8[5971968]{0:T(1024)(128)(4,1)} %bitcast.202), calls=%async_computation.12 | async-start | bytes 8388608
  459.0 16.4 %slice-start.3 = ((s8[5971968]{0:T(1024)(128)(4,1)}), s8[1777664]{0:T(1024)(128)(4,1)S(1)}, s32[]{:S(2)}) async-start(s8[5971968]{0:T(1024)(128)(4,1)} %bitcast.196), calls=%async_computation.7 | async-start | bytes 3555328
  459.0 16.4 %slice-start.5 = ((s8[5971968]{0:T(1024)(128)(4,1)}), s8[1777664]{0:T(1024)(128)(4,1)S(1)}, s32[]{:S(2)}) async-start(s8[5971968]{0:T(1024)(128)(4,1)} %bitcast.198), calls=%async_computation.9 | async-start | bytes 3555328
  459.0 16.4 %slice-start.9 = ((s8[5971968]{0:T(1024)(128)(4,1)}), s8[1777664]{0:T(1024)(128)(4,1)S(1)}, s32[]{:S(2)}) async-start(s8[5971968]{0:T(1024)(128)(4,1)} %bitcast.202), calls=%async_computation.13 | async-start | bytes 3555328
  459.0 16.4 %copy-start.17 = (f32[3,256,768]{2,1,0:T(8,128)S(1)}, f32[3,256,768]{2,1,0:T(8,128)}, u32[]{:S(2)}) copy-start(f32[3,256,768]{2,1,0:T(8,128)} %rev.9) | copy-start | bytes 7077892
  472.7 104.0 %collective-permute-start.1 = (bf16[3,2,2304]{2,1,0:T(2,128)(2,1)}, bf16[3,2,2304]{2,1,0:T(2,128)(2,1)}, u32[]{:S(2)}, u32[]{:S(2)}) collective-permute-start(bf16[3,2,2304]{2,1,0:T(2,128)(2,1)} %slice.121), channel_id=1, source_target_pairs={{8,0},{16,8},{24,16},{9,1},{17,9},{25,17},{10,2},{18,10},{26,18},{... | collective-permute-start | bytes 82952 | tf_op jit(solution)/shard_map/ppermute | solution.py:17
  541.6 10.6 copy-start.86
  552.2 12.0 copy-start.38
  552.2 13.0 %copy-start.44 = (f32[1024,64]{0,1:T(8,128)S(1)}, f32[1024,64]{0,1:T(8,128)}, u32[]{:S(2)}) copy-start(f32[1024,64]{0,1:T(8,128)} %get-tuple-element.98) | copy-start | bytes 786436
  552.2 17.7 %copy-start.20 = (f32[1024,768]{1,0:T(8,128)S(1)}, f32[1024,768]{1,0:T(8,128)}, u32[]{:S(2)}) copy-start(f32[1024,768]{1,0:T(8,128)} %get-tuple-element.102) | copy-start | bytes 9437188
  557.5 10.5 copy-start.43
  557.5 10.5 copy-start.60
  557.5 12.4 %copy-start.18 = (f32[2048,768]{1,0:T(8,128)S(1)}, f32[2048,768]{1,0:T(8,128)}, u32[]{:S(2)}) copy-start(f32[2048,768]{1,0:T(8,128)} %dynamic_update_slice.3) | copy-start | bytes 18874372
  584.6 606.3 %all-reduce.14.cloned.1.call-start = ((), (), s32[]{:S(2)}) async-start(), calls=%async_computation.3 | async-start | bytes 57016320 | tf_op jit(solution)/shard_map/psum | solution.py:298
  1193.5 10.2 copy-start.113
  1193.5 10.7 copy-start.87
  1193.5 11.3 copy-start.112
  1193.5 11.8 copy-start.56
  1193.5 12.5 %copy-start.107 = (f32[768]{0:T(1024)S(1)}, f32[768]{0:T(1024)}, u32[]{:S(2)}) copy-start(f32[768]{0:T(1024)} %get-tuple-element.134) | copy-start | bytes 9220
  1193.5 13.1 %copy-start.106 = (f32[768]{0:T(1024)S(1)}, f32[768]{0:T(1024)}, u32[]{:S(2)}) copy-start(f32[768]{0:T(1024)} %get-tuple-element.135) | copy-start | bytes 9220
  1193.5 13.7 %copy-start.34 = (f32[768,768]{1,0:T(8,128)S(1)}, f32[768,768]{1,0:T(8,128)}, u32[]{:S(2)}) copy-start(f32[768,768]{1,0:T(8,128)} %get-tuple-element.136) | copy-start | bytes 7077892
  1200.1 9.7 copy-start.103
  1207.2 12.6 %slice-start.10 = ((s8[9437184]{0:T(1024)(128)(4,1)}), s8[4194304]{0:T(1024)(128)(4,1)S(1)}, s32[]{:S(2)}) async-start(s8[9437184]{0:T(1024)(128)(4,1)} %bitcast.204), calls=%async_computation.14 | async-start | bytes 8388608
  (72 other events, 365.6 us)
Sparse Core Ops, SparseCore 0:
  33.1 41.5 all-gather.2
  240.1 41.6 all-gather.4
  584.7 158.1 all-reduce.11
  750.9 439.9 all-reduce.13
where the time goes:
time: 1240 us; the launch traced here: 1230 us
  waiting for transfers between devices  585 us (47%)
  matrix products  438 us (35%)
  local copies, waits for them, and re-layouts  122 us (10%)
  other arithmetic  65.6 us (5%)
  between operations  15.5 us (1%)
    psum x2, waiting for transfers between devices, shards(): lax.psum((grad_norm1_gain, grad_norm1_shift, grad_in_weight, grad_in_bias...  585 us
    dot_general x3, matrix products, rows_back(): jnp.einsum('tf,bfk->btk', inv_sin, imag_part, precision=highest)  63.5 us
    dot_general x3, matrix products, rows_spectrum(): real_part = jnp.einsum('ft,btk->bfk', cos_table, values, precision=highest)  57.1 us
    dot_general x3, matrix products, rows_spectrum(): imag_part = -jnp.einsum('ft,btk->bfk', sin_table, values, precision=highest)  55.1 us
    dot_general x3, matrix products, rows_back(): jnp.einsum('tf,bfk->btk', inv_cos, real_part, precision=highest)  51.6 us
    dot_general x2, matrix products, window_spectrum(): real_part = jnp.einsum('ft,tk->fk', cos_table, window, precision=highest)  46.9 us
    dot_general x2, matrix products, window_spectrum(): imag_part = -jnp.einsum('ft,tk->fk', sin_table, window, precision=highest)  45.4 us
    unnamed x283, local copies, waits for them, and re-layouts  45.1 us
  transfers between devices with their start and end apart: 6, of which 2 were waited for; matrix products, arithmetic and copies ran while one was open for 26% of the time, Pallas kernels for 0%

commit v1 on v0

v1 whole, which is shorter than its diff:
```python
from functools import partial
import math

import jax
import jax.numpy as jnp
import numpy as np
from jax import lax
from jax.experimental import pallas as pl
from jax.experimental.pallas import tpu as pltpu
from jax.sharding import PartitionSpec as P

norm_eps = 1e-05
window_floor = 0.05
highest = lax.Precision.HIGHEST
HALO = 16
bf16 = jnp.bfloat16
f32 = jnp.float32


def dot(a, b, ca=1, cb=0, precision=None):
    return lax.dot_general(
        a, b, (((ca,), (cb,)), ((), ())), precision=precision, preferred_element_type=f32
    )


def xor_permute(array, axis, bit):
    count = lax.axis_size(axis)
    return lax.ppermute(array, axis, [(i, i ^ bit) for i in range(count)])


def exchange_seq(array):
    count = lax.axis_size("seq")
    held = {0: array}
    bit = count // 2
    while bit:
        held.update({k ^ bit: xor_permute(a, "seq", bit) for k, a in list(held.items())})
        bit //= 2
    return [held[k] for k in range(count)]


def block_tables(rows):
    phase = (2 * np.arange(rows)[:, None] + 1) * np.arange(rows)[None, :] % (4 * rows)
    angle = phase * (2.0 * math.pi / (4 * rows))
    table = np.concatenate([np.cos(angle), -np.sin(angle)], axis=0)
    high = table.astype(jnp.bfloat16)
    low = (table - high.astype(np.float64)).astype(jnp.bfloat16)
    return high, low


def features(seq_total, emb_width):
    bands = (emb_width - 1) // 2
    steps = np.arange(seq_total)
    phases = steps[:, None] * np.arange(1, bands + 1)[None, :] % seq_total
    angles = phases * (2.0 * math.pi / seq_total)
    ramp = steps / seq_total
    return np.concatenate([ramp[:, None], np.cos(angles), np.sin(angles)], axis=1).astype(np.float32)


def filter_hidden(table, filter_in, in_bias, filter_mid, mid_bias, filter_last, last_bias):
    hidden = jnp.sin(jnp.dot(table, filter_in, precision=highest) + in_bias)
    hidden = jnp.sin(jnp.dot(hidden, filter_mid, precision=highest) + mid_bias)
    return jnp.sin(jnp.dot(hidden, filter_last, precision=highest) + last_bias)


def normalized(values):
    center = values - jnp.mean(values, axis=-1, keepdims=True)
    scale = lax.rsqrt(jnp.mean(center * center, axis=-1, keepdims=True) + norm_eps)
    return center * scale, scale


def live_rows(meta, bucket, rows):
    place = meta[0] * rows + lax.broadcasted_iota(jnp.int32, (rows, 1), 0)
    return (place < meta[1 + bucket]).astype(f32)


def params(mib, count=1):
    return pltpu.CompilerParams(
        dimension_semantics=("arbitrary",) * count, vmem_limit_bytes=mib * 1024 * 1024
    )


SMEM = pl.BlockSpec(memory_space=pltpu.SMEM)


def whole(shape):
    zeros = (0,) * len(shape)
    return pl.BlockSpec(tuple(shape), lambda *_: zeros)


def cost(flops, read):
    return pl.CostEstimate(flops=flops, bytes_accessed=read, transcendentals=0)


def front_body(buckets, rows, meta, tok, halo, gain, shift, w0, w1, w2, bias, cw, cb,
               normed, mixed, product, gate_out, taps_in):
    ext = rows + HALO

    @pl.when(pl.program_id(0) == 0)
    def _():
        for b in range(buckets):
            hat, _ = normalized(halo[b].astype(f32))
            normed[b * ext : b * ext + HALO] = (hat * gain[...] + shift[...]).astype(bf16)
            hat, _ = normalized(tok[b].astype(f32))
            normed[b * ext + HALO : (b + 1) * ext] = (hat * gain[...] + shift[...]).astype(bf16)

    inner = meta[0] > 0
    for b in range(buckets):
        parts = []
        for t, w in enumerate((w0, w1, w2)):
            m = (dot(normed[b * ext : (b + 1) * ext], w[...]) + bias[t : t + 1]).astype(bf16)
            head = jnp.where(inner, m[:HALO].astype(f32), 0.0)
            mixed[t, b, :HALO] = head.astype(bf16)
            mixed[t, b, HALO:] = m[HALO:]
            taps_in[t, :HALO] = head
            taps_in[t, HALO:] = m[HALO:].astype(f32)
            s = cb[t : t + 1]
            for i in range(3):
                s = s + cw[i, t : t + 1] * taps_in[t, HALO - 2 + i : HALO - 2 + i + rows]
            parts.append(s)
        gate_out[b] = parts[0]
        product[b] = (parts[2] * parts[1] * live_rows(meta, b, rows)).astype(bf16)


def front(meta, tok, halo, gain, shift, in_weight, in_bias, conv_weight, conv_bias):
    buckets, rows, width = tok.shape
    ext = rows + HALO
    tile = 256
    steps = width // tile
    columns = [pl.BlockSpec((width, tile), lambda c, t=t: (0, t * steps + c)) for t in range(3)]
    return pl.pallas_call(
        partial(front_body, buckets, rows),
        grid=(steps,),
        in_specs=[
            SMEM, whole(tok.shape), whole(halo.shape), whole((1, width)), whole((1, width)), *columns,
            pl.BlockSpec((3, tile), lambda c: (0, c)),
            pl.BlockSpec((3, 3, tile), lambda c: (0, 0, c)),
            pl.BlockSpec((3, tile), lambda c: (0, c)),
        ],
        out_specs=[
            whole((buckets * ext, width)),
            pl.BlockSpec((3, buckets, ext, tile), lambda c: (0, 0, 0, c)),
            pl.BlockSpec((buckets, rows, tile), lambda c: (0, 0, c)),
            pl.BlockSpec((buckets, rows, tile), lambda c: (0, 0, c)),
        ],
        out_shape=[
            jax.ShapeDtypeStruct((buckets * ext, width), bf16),
            jax.ShapeDtypeStruct((3, buckets, ext, width), bf16),
            jax.ShapeDtypeStruct((buckets, rows, width), bf16),
            jax.ShapeDtypeStruct((buckets, rows, width), f32),
        ],
        scratch_shapes=[pltpu.VMEM((3, ext, tile), f32)],
        compiler_params=params(48),
        cost_estimate=cost(6 * buckets * ext * width * width, 16 << 20),
        name="front",
    )(meta, tok, halo, gain, shift, in_weight, in_weight, in_weight, in_bias, conv_weight, conv_bias)


def alternating(rows):
    parity = lax.broadcasted_iota(jnp.int32, (rows, 1), 0) % 2
    return (1 - 2 * parity).astype(f32)


def window_of(first, rows, total, decay):
    ramp = (first + lax.broadcasted_iota(jnp.int32, (rows, 1), 0)).astype(f32) * (1.0 / total)
    return ramp, jnp.exp(-ramp * decay)


def filter_body(blocks, rows, hidden, out, decay, high, low, shaped, spectrum):
    sign = alternating(rows)
    last = None
    for m in range(blocks):
        here = slice(m * rows, (m + 1) * rows)
        plain = dot(hidden[here], out[...], precision=highest)
        shaped[here] = plain
        _, fall = window_of(m * rows, rows, blocks * rows, decay[...])
        taps = plain * (fall + window_floor)
        upper = taps.astype(bf16)
        rest = (taps - upper.astype(f32)).astype(bf16)
        full = dot(high[...], upper) + (dot(high[...], rest) + dot(low[...], upper))
        re, im = full[:rows], full[rows:]
        if last is None:
            spectrum[m, :rows] = re
            spectrum[m, rows:] = im
        else:
            spectrum[m, :rows] = re - sign * last[1]
            spectrum[m, rows:] = im + sign * last[0]
        last = (re, im)


def filter_spectra(hidden, filter_out, decay, high, low, blocks):
    total, inner = hidden.shape
    width = filter_out.shape[1]
    rows = total // blocks
    tile = 256
    return pl.pallas_call(
        partial(filter_body, blocks, rows),
        grid=(width // tile,),
        in_specs=[
            whole(hidden.shape),
            pl.BlockSpec((inner, tile), lambda c: (0, c)),
            pl.BlockSpec((1, tile), lambda c: (0, c)),
            whole(high.shape), whole(low.shape),
        ],
        out_specs=[
            pl.BlockSpec((total, tile), lambda c: (0, c)),
            pl.BlockSpec((blocks, 2 * rows, tile), lambda c: (0, 0, c)),
        ],
        out_shape=[
            jax.ShapeDtypeStruct((total, width), f32),
            jax.ShapeDtypeStruct((blocks, 2 * rows, width), f32),
        ],
        compiler_params=params(48),
        cost_estimate=cost(20 * total * width * rows, 10 << 20),
        name="filter_spectra",
    )(hidden, filter_out, decay, high, low)


def conv_body(blocks, rows, meta, *refs):
    products = refs[:blocks]
    spectrum, gate_out, skip, high, back, mixture, gated, total = refs[blocks:]
    own = meta[0]
    for k in range(blocks):
        lag = own - (own ^ k)

        def add(k=k, lag=lag):
            full = dot(high[...], products[k][0])
            re, im = full[:rows], full[rows:]
            tap_re, tap_im = spectrum[lag, :rows], spectrum[lag, rows:]
            out_re = tap_re * re - tap_im * im
            out_im = tap_re * im + tap_im * re
            if k == 0:
                total[:rows] = out_re
                total[rows:] = out_im
            else:
                total[:rows] += out_re
                total[rows:] += out_im

        if k == 0:
            add()
        else:
            pl.when(lag >= 0)(add)
    convolved = dot(back[...], total[...].astype(bf16)) * (1.0 / rows)
    mixed = convolved + skip[...] * products[0][0].astype(f32)
    mixture[0] = mixed
    gated[0] = (mixed * gate_out[0]).astype(bf16)


def conv_forward(meta, products, spectrum, gate_out, skip, high, back):
    buckets, rows, width = gate_out.shape
    blocks = len(products)
    tile = 256
    piece = pl.BlockSpec((1, rows, tile), lambda c, b: (b, 0, c))
    return pl.pallas_call(
        partial(conv_body, blocks, rows),
        grid=(width // tile, buckets),
        in_specs=[SMEM] + [piece] * blocks + [
            pl.BlockSpec((blocks, 2 * rows, tile), lambda c, b: (0, 0, c)),
            piece,
            pl.BlockSpec((1, tile), lambda c, b: (0, c)),
            whole(high.shape), whole(back.shape),
        ],
        out_specs=[piece, piece],
        out_shape=[
            jax.ShapeDtypeStruct((buckets, rows, width), f32),
            jax.ShapeDtypeStruct((buckets, rows, width), bf16),
        ],
        scratch_shapes=[pltpu.VMEM((2 * rows, tile), f32)],
        compiler_params=params(48, 2),
        cost_estimate=cost(4 * (blocks + 1) * rows * rows * width * buckets, 16 << 20),
        name="conv_forward",
    )(meta, *products, spectrum, gate_out, skip, high, back)


def gelu_parts(u):
    cdf = 0.5 + 0.5 * lax.erf(u * (1.0 / math.sqrt(2.0)))
    pdf = jnp.exp(-0.5 * u * u) * (1.0 / math.sqrt(2.0 * math.pi))
    return u * cdf, cdf + u * pdf


def middle_body(buckets, rows, steps, meta, gated, out_w, out_b, tok, cot, gain, shift, up_w, up_b, down_w,
                gate_out, normed2, d_down, resid, active, d_up, g_up_bias, d_resid, d_mixer, d_gated, d_conv,
                g_gain, g_shift, g_out_bias, total):
    step = pl.program_id(0)

    @pl.when(step == 0)
    def _():
        for b in range(buckets):
            here = slice(b * rows, (b + 1) * rows)
            live = live_rows(meta, b, rows)
            mixer = dot(gated[here], out_w[...]) + out_b[...]
            r = tok[here].astype(f32) + live * mixer
            resid[here] = r
            hat, _ = normalized(r)
            normed2[here] = (hat * gain[...] + shift[...]).astype(bf16)
            d_down[here] = (live * cot[here].astype(f32)).astype(bf16)

    bias_sum = None
    for b in range(buckets):
        here = slice(b * rows, (b + 1) * rows)
        u = dot(normed2[here], up_w[...]) + up_b[...]
        d_active = dot(d_down[here], down_w[...], 1, 1)
        act, slope = gelu_parts(u)
        active[here] = act.astype(bf16)
        d_u = (d_active * slope).astype(bf16)
        d_up[here] = d_u
        part = jnp.sum(d_u.astype(f32), axis=0, keepdims=True)
        bias_sum = part if bias_sum is None else bias_sum + part
        back = dot(d_u, up_w[...], 1, 1)

        @pl.when(step == 0)
        def _(back=back, here=here):
            total[here] = back

        @pl.when(step > 0)
        def _(back=back, here=here):
            total[here] += back

    g_up_bias[...] = bias_sum

    @pl.when(step == steps - 1)
    def _():
        sums = [jnp.zeros((1, gain.shape[1]), f32)] * 3
        for b in range(buckets):
            here = slice(b * rows, (b + 1) * rows)
            live = live_rows(meta, b, rows)
            hat, scale = normalized(resid[here])
            d = total[here]
            sums[0] = sums[0] + jnp.sum(d * hat, axis=0, keepdims=True)
            sums[1] = sums[1] + jnp.sum(d, axis=0, keepdims=True)
            e = d * gain[...]
            mean_e = jnp.mean(e, axis=-1, keepdims=True)
            mean_eh = jnp.mean(e * hat, axis=-1, keepdims=True)
            d_r = cot[here].astype(f32) + (e - mean_e - hat * mean_eh) * scale
            d_resid[here] = d_r
            d_m = (live * d_r).astype(bf16)
            d_mixer[here] = d_m
            sums[2] = sums[2] + jnp.sum(d_m.astype(f32), axis=0, keepdims=True)
            d_g = dot(d_m, out_w[...], 1, 1)
            d_gated[here] = d_g
            d_conv[here] = (d_g * gate_out[here]).astype(bf16)
        g_gain[...] = sums[0]
        g_shift[...] = sums[1]
        g_out_bias[...] = sums[2]


def middle(meta, gated, out_w, out_b, tok, cot, gain, shift, up_w, up_b, down_w, gate_out, buckets):
    count, width = tok.shape
    hidden = up_w.shape[1]
    tile = 384
    steps = hidden // tile
    rows = count // buckets
    square = whole((count, width))
    line = whole((1, width))
    shape = jax.ShapeDtypeStruct
    return pl.pallas_call(
        partial(middle_body, buckets, rows, steps),
        grid=(steps,),
        in_specs=[
            SMEM, square, whole(out_w.shape), line, square, square, line, line,
            pl.BlockSpec((width, tile), lambda s: (0, s)),
            pl.BlockSpec((1, tile), lambda s: (0, s)),
            pl.BlockSpec((tile, width), lambda s: (s, 0)),
            square,
        ],
        out_specs=[
            square, square, square,
            pl.BlockSpec((count, tile), lambda s: (0, s)),
            pl.BlockSpec((count, tile), lambda s: (0, s)),
            pl.BlockSpec((1, tile), lambda s: (0, s)),
            square, square, square, square, line, line, line,
        ],
        out_shape=[
            shape((count, width), bf16), shape((count, width), bf16), shape((count, width), f32),
            shape((count, hidden), bf16), shape((count, hidden), bf16), shape((1, hidden), f32),
            shape((count, width), f32), shape((count, width), bf16), shape((count, width), f32),
            shape((count, width), bf16), shape((1, width), f32), shape((1, width), f32), shape((1, width), f32),
        ],
        scratch_shapes=[pltpu.VMEM((count, width), f32)],
        compiler_params=params(56),
        cost_estimate=cost(6 * count * width * hidden, 40 << 20),
        name="middle",
    )(meta, gated, out_w, out_b, tok, cot, gain, shift, up_w, up_b, down_w, gate_out)


def weights_body(buckets, rows, steps, meta, active, d_up, normed2, d_down, down_w, down_b, resid, gated, d_mixer,
                 block_out, g_down, g_up, g_out, g_down_bias, total):
    step = pl.program_id(0)
    part = dot(active[...], down_w[...])

    @pl.when(step == 0)
    def _():
        total[...] = part
        g_out[...] = dot(gated[...], d_mixer[...], 0, 0).astype(bf16)
        g_down_bias[...] = jnp.sum(d_down[...].astype(f32), axis=0, keepdims=True)

    @pl.when(step > 0)
    def _():
        total[...] += part

    g_down[...] = dot(active[...], d_down[...], 0, 0).astype(bf16)
    g_up[0] = dot(normed2[...], d_up[...], 0, 0).astype(bf16)

    @pl.when(step == steps - 1)
    def _():
        for b in range(buckets):
            here = slice(b * rows, (b + 1) * rows)
            live = live_rows(meta, b, rows)
            block_out[here] = (resid[here] + live * (total[here] + down_b[...])).astype(bf16)


def weight_grads(meta, active, d_up, normed2, d_down, down_w, down_b, resid, gated, d_mixer, buckets):
    count, width = normed2.shape
    hidden = down_w.shape[0]
    tile = 384
    steps = hidden // tile
    per = width // tile
    rows = count // buckets
    square = whole((count, width))
    shape = jax.ShapeDtypeStruct
    return pl.pallas_call(
        partial(weights_body, buckets, rows, steps),
        grid=(steps,),
        in_specs=[
            SMEM,
            pl.BlockSpec((count, tile), lambda s: (0, s)),
            pl.BlockSpec((count, tile), lambda s: (0, s)),
            square, square,
            pl.BlockSpec((tile, width), lambda s: (s, 0)),
            whole((1, width)), square, square, square,
        ],
        out_specs=[
            square,
            pl.BlockSpec((tile, width), lambda s: (s, 0)),
            pl.BlockSpec((1, width, tile), lambda s: (s // per, 0, s % per)),
            whole((width, width)),
            whole((1, width)),
        ],
        out_shape=[
            shape((count, width), bf16), shape((hidden, width), bf16),
            shape((hidden // width, width, width), bf16),
            shape((width, width), bf16), shape((1, width), f32),
        ],
        scratch_shapes=[pltpu.VMEM((count, width), f32)],
        compiler_params=params(56),
        cost_estimate=cost(6 * count * width * hidden, 40 << 20),
        name="weight_grads",
    )(meta, active, d_up, normed2, d_down, down_w, down_b, resid, gated, d_mixer)


def conv_back_body(blocks, rows, buckets, meta, *refs):
    grads = refs[:blocks]
    (product, spectrum, skip, high, back, hidden, filter_out, decay, shaped,
     d_product, g_hidden, g_filter_out, g_decay, g_skip, total, lags) = refs[blocks:]
    own = meta[0]
    tile_step, b = pl.program_id(0), pl.program_id(1)

    @pl.when(b == 0)
    def _():
        lags[...] = jnp.zeros_like(lags)
        g_skip[...] = jnp.zeros_like(g_skip)

    full = dot(high[...], product[0])
    prod_re, prod_im = full[:rows], full[rows:]
    for k in range(blocks):
        lag = (own ^ k) - own

        def add(k=k, lag=lag):
            grad = dot(high[...], grads[k][0])
            re, im = grad[:rows], grad[rows:]
            tap_re, tap_im = spectrum[lag, :rows], spectrum[lag, rows:]
            out_re = tap_re * re + tap_im * im
            out_im = tap_re * im - tap_im * re
            if k == 0:
                total[:rows] = out_re
                total[rows:] = out_im
            else:
                total[:rows] += out_re
                total[rows:] += out_im
            lags[lag, :rows] += re * prod_re + im * prod_im
            lags[lag, rows:] += im * prod_re - re * prod_im

        if k == 0:
            add()
        else:
            pl.when(lag >= 0)(add)
    d_own = grads[0][0].astype(f32)
    d_product[0] = dot(back[...], total[...].astype(bf16)) * (1.0 / rows) + skip[...] * d_own
    g_skip[...] += jnp.sum(d_own * product[0].astype(f32), axis=0, keepdims=True)

    @pl.when(b == buckets - 1)
    def _():
        sign = alternating(rows)
        sum_out = jnp.zeros(g_filter_out.shape, f32)
        sum_decay = jnp.zeros(g_decay.shape, f32)
        for m in range(blocks):
            here = slice(m * rows, (m + 1) * rows)
            re, im = lags[m, :rows], lags[m, rows:]
            if m + 1 < blocks:
                re, im = re + sign * lags[m + 1, rows:], im - sign * lags[m + 1, :rows]
            d_taps = (dot(back[:, :rows], re.astype(bf16)) + dot(back[:, rows:], im.astype(bf16))) * (1.0 / rows)
            ramp, fall = window_of(m * rows, rows, blocks * rows, decay[...])
            sum_decay = sum_decay - jnp.sum(d_taps * shaped[here] * ramp * fall, axis=0, keepdims=True)
            d_shaped = (d_taps * (fall + window_floor)).astype(bf16)
            sum_out = sum_out + dot(hidden[here], d_shaped, 0, 0)
            d_hidden = dot(d_shaped, filter_out[...], 1, 1)

            @pl.when(tile_step == 0)
            def _(d_hidden=d_hidden, here=here):
                g_hidden[here] = d_hidden

            @pl.when(tile_step > 0)
            def _(d_hidden=d_hidden, here=here):
                g_hidden[here] += d_hidden

        g_filter_out[...] = sum_out
        g_decay[...] = sum_decay


def conv_backward(meta, grads, product, spectrum, skip, high, back, hidden, filter_out, decay, shaped):
    buckets, rows, width = product.shape
    blocks = len(grads)
    total, inner = hidden.shape
    tile = 256
    piece = pl.BlockSpec((1, rows, tile), lambda c, b: (b, 0, c))
    line = pl.BlockSpec((1, tile), lambda c, b: (0, c))
    shape = jax.ShapeDtypeStruct
    return pl.pallas_call(
        partial(conv_back_body, blocks, rows, buckets),
        grid=(width // tile, buckets),
        in_specs=[SMEM] + [piece] * blocks + [
            piece,
            pl.BlockSpec((blocks, 2 * rows, tile), lambda c, b: (0, 0, c)),
            line, whole(high.shape), whole(back.shape), whole(hidden.shape),
            pl.BlockSpec((inner, tile), lambda c, b: (0, c)),
            line,
            pl.BlockSpec((total, tile), lambda c, b: (0, c)),
        ],
        out_specs=[
            piece, whole((total, inner)),
            pl.BlockSpec((inner, tile), lambda c, b: (0, c)),
            line, line,
        ],
        out_shape=[
            shape((buckets, rows, width), f32), shape((total, inner), f32), shape((inner, width), f32),
            shape((1, width), f32), shape((1, width), f32),
        ],
        scratch_shapes=[pltpu.VMEM((2 * rows, tile), f32), pltpu.VMEM((blocks, 2 * rows, tile), f32)],
        compiler_params=params(48, 2),
        cost_estimate=cost(4 * (2 * blocks + 2) * rows * rows * width * buckets, 20 << 20),
        name="conv_backward",
    )(meta, *grads, product, spectrum, skip, high, back, hidden, filter_out, decay, shaped)


def tail_body(buckets, rows, steps, meta, mixed, d_product, mixture, d_gated, normed, w0, w1, w2, cw, cb,
              tok, halo, gain, d_resid, g_tokens, d_halo, g_in, g_conv, g_conv_bias, g_bias, g_gain, g_shift,
              taps_in, d_pad, g_mixed, total):
    ext = rows + HALO
    step = pl.program_id(0)
    inner = meta[0] > 0
    tile = cb.shape[1]
    sums = [[jnp.zeros((1, tile), f32)] * 5 for _ in range(3)]
    for b in range(buckets):
        live = live_rows(meta, b, rows)
        short = []
        for t in range(3):
            taps_in[t] = mixed[t, b].astype(f32)
            s = cb[t : t + 1]
            if t:
                for i in range(3):
                    s = s + cw[i, t : t + 1] * taps_in[t, HALO - 2 + i : HALO - 2 + i + rows]
            short.append(s)
        d_prod = d_product[b] * live
        d_shorts = (d_gated[b] * mixture[b], d_prod * short[2], d_prod * short[1])
        for t in range(3):
            d_short = d_shorts[t]
            d_pad[t, :HALO] = jnp.zeros((HALO, tile), f32)
            d_pad[t, HALO : HALO + rows] = d_short
            d_pad[t, HALO + rows :] = jnp.zeros((8, tile), f32)
            for i in range(3):
                sums[t][i] = sums[t][i] + jnp.sum(
                    d_short * taps_in[t, HALO - 2 + i : HALO - 2 + i + rows], axis=0, keepdims=True)
            sums[t][3] = sums[t][3] + jnp.sum(d_short, axis=0, keepdims=True)
            g = (cw[2, t : t + 1] * d_pad[t, :ext] + cw[1, t : t + 1] * d_pad[t, 1 : ext + 1]
                 + cw[0, t : t + 1] * d_pad[t, 2 : ext + 2])
            head = jnp.where(inner, g[:HALO], 0.0).astype(bf16)
            body = g[HALO:].astype(bf16)
            g_mixed[t, b * ext : b * ext + HALO] = head
            g_mixed[t, b * ext + HALO : (b + 1) * ext] = body
            sums[t][4] = sums[t][4] + (jnp.sum(head.astype(f32), axis=0, keepdims=True)
                                       + jnp.sum(body.astype(f32), axis=0, keepdims=True))
    for t, w in enumerate((w0, w1, w2)):
        for i in range(3):
            g_conv[i, t : t + 1] = sums[t][i]
        g_conv_bias[t : t + 1] = sums[t][3]
        g_bias[t : t + 1] = sums[t][4]
        g_in[t] = dot(normed[...], g_mixed[t], 0, 0).astype(bf16)
    back = dot(g_mixed[0], w0[...], 1, 1) + dot(g_mixed[1], w1[...], 1, 1) + dot(g_mixed[2], w2[...], 1, 1)

    @pl.when(step == 0)
    def _():
        total[...] = back

    @pl.when(step > 0)
    def _():
        total[...] += back

    @pl.when(step == steps - 1)
    def _():
        add = [jnp.zeros((1, gain.shape[1]), f32)] * 2
        for b in range(buckets):
            for first, size, source in ((0, HALO, halo), (HALO, rows, tok)):
                d = total[b * ext + first : b * ext + first + size]
                hat, scale = normalized(source[b].astype(f32))
                add[0] = add[0] + jnp.sum(d * hat, axis=0, keepdims=True)
                add[1] = add[1] + jnp.sum(d, axis=0, keepdims=True)
                e = d * gain[...]
                mean_e = jnp.mean(e, axis=-1, keepdims=True)
                mean_eh = jnp.mean(e * hat, axis=-1, keepdims=True)
                d_v = (e - mean_e - hat * mean_eh) * scale
                if first:
                    g_tokens[b] = d_resid[b] + d_v
                else:
                    d_halo[b] = d_v
        g_gain[...] = add[0]
        g_shift[...] = add[1]


def tail(meta, mixed, d_product, mixture, d_gated, normed, in_weight, conv_weight, conv_bias, tok, halo, gain, d_resid):
    buckets, rows, width = tok.shape
    ext = rows + HALO
    tile = 256
    steps = width // tile
    columns = [pl.BlockSpec((width, tile), lambda c, t=t: (0, t * steps + c)) for t in range(3)]
    piece = pl.BlockSpec((buckets, rows, tile), lambda c: (0, 0, c))
    three = pl.BlockSpec((3, tile), lambda c: (0, c))
    nine = pl.BlockSpec((3, 3, tile), lambda c: (0, 0, c))
    shape = jax.ShapeDtypeStruct
    return pl.pallas_call(
        partial(tail_body, buckets, rows, steps),
        grid=(steps,),
        in_specs=[
            SMEM,
            pl.BlockSpec((3, buckets, ext, tile), lambda c: (0, 0, 0, c)),
            piece, piece, piece, whole(normed.shape), *columns, nine, three,
            whole(tok.shape), whole(halo.shape), whole((1, width)), whole(tok.shape),
        ],
        out_specs=[
            whole(tok.shape), whole(halo.shape),
            pl.BlockSpec((3, width, tile), lambda c: (0, 0, c)),
            nine, three, three, whole((1, width)), whole((1, width)),
        ],
        out_shape=[
            shape(tok.shape, f32), shape(halo.shape, f32), shape((3, width, width), bf16),
            shape((3, 3, width), f32), shape((3, width), f32), shape((3, width), f32),
            shape((1, width), f32), shape((1, width), f32),
        ],
        scratch_shapes=[
            pltpu.VMEM((3, ext, tile), f32),
            pltpu.VMEM((3, ext + 8, tile), f32),
            pltpu.VMEM((3, buckets * ext, tile), bf16),
            pltpu.VMEM((buckets * ext, width), f32),
        ],
        compiler_params=params(56),
        cost_estimate=cost(12 * buckets * ext * width * width, 30 << 20),
        name="tail",
    )(meta, mixed, d_product, mixture, d_gated, normed, in_weight, in_weight, in_weight, conv_weight, conv_bias,
      tok, halo, gain, d_resid)


def index_bits(axis):
    count = lax.axis_size(axis)
    return [(axis, 1 << i) for i in range(count.bit_length() - 1)]


def bit_of(axis, bit):
    return (lax.axis_index(axis) // bit) % 2


def scatter_sum(array, order):
    for axis, bit in order:
        half = array.shape[0] // 2
        mine = bit_of(axis, bit)
        sent = lax.dynamic_slice_in_dim(array, (1 - mine) * half, half, 0)
        kept = lax.dynamic_slice_in_dim(array, mine * half, half, 0)
        array = (kept.astype(f32) + xor_permute(sent, axis, bit).astype(f32)).astype(bf16)
    return array


def gather_rows(array, order):
    for axis, bit in reversed(order):
        other = xor_permute(array, axis, bit)
        high = bit_of(axis, bit) == 1
        array = jnp.concatenate([jnp.where(high, other, array), jnp.where(high, array, other)], axis=0)
    return array


def unscramble(gathered, order):
    names = [b for axis in ("seq", "batch") for b in reversed(index_bits(axis))]
    rows, width = gathered.shape[1:]
    cube = gathered.reshape([2] * len(names) + [rows, width])
    places = [names.index(b) for b in order] + [len(names), len(names) + 1]
    return cube.transpose(places).reshape(gathered.shape[0] * rows, width)


def shards(
    tokens, cotangent, lengths, norm1_gain, norm1_shift, in_weight, in_bias, conv_weight, conv_bias,
    filter_in, filter_in_bias, filter_mid, filter_mid_bias, filter_last, filter_last_bias, filter_out,
    decay_rate, skip_gain, out_weight, out_bias, norm2_gain, norm2_shift, up_weight, up_bias,
    down_weight, down_bias,
):
    buckets, rows, width = tokens.shape
    hidden_width = up_weight.shape[1]
    blocks = lax.axis_size("seq")
    devices = blocks * lax.axis_size("batch")
    count = buckets * rows
    meta = jnp.concatenate([lax.axis_index("seq")[None].astype(jnp.int32), lengths.astype(jnp.int32)])
    high_np, low_np = block_tables(rows)
    high, low = jnp.asarray(high_np), jnp.asarray(low_np)
    back = jnp.asarray(np.ascontiguousarray(high_np.T))
    line = lambda a: a.reshape(1, -1)

    halo = lax.ppermute(tokens[:, rows - HALO :], "seq", [(i, i + 1) for i in range(blocks - 1)])
    conv_w = conv_weight.reshape(3, 3, width)
    conv_b = conv_bias.reshape(3, width)
    normed, mixed, product, gate_out = front(
        meta, tokens, halo, line(norm1_gain), line(norm1_shift), in_weight, in_bias.reshape(3, width), conv_w, conv_b)
    products = exchange_seq(product)
    table = jnp.asarray(features(rows * blocks, filter_in.shape[0]))
    hidden, hidden_pull = jax.vjp(
        partial(filter_hidden, table), filter_in, filter_in_bias, filter_mid, filter_mid_bias,
        filter_last, filter_last_bias)
    shaped, spectrum = filter_spectra(hidden, filter_out, line(decay_rate), high, low, blocks)
    mixture, gated = conv_forward(meta, products, spectrum, gate_out, line(skip_gain), high, back)

    flat = lambda a: a.reshape(count, width)
    (normed2, d_down, resid, active, d_up, g_up_bias, d_resid, d_mixer, d_gated, d_conv,
     g_norm2_gain, g_norm2_shift, g_out_bias) = middle(
        meta, flat(gated), out_weight, line(out_bias), flat(tokens), flat(cotangent), line(norm2_gain),
        line(norm2_shift), up_weight, line(up_bias), down_weight, flat(gate_out), buckets)
    cube = lambda a: a.reshape(buckets, rows, width)
    grads = exchange_seq(cube(d_conv))
    block_out, g_down, g_up, g_out, g_down_bias = weight_grads(
        meta, active, d_up, normed2, d_down, down_weight, line(down_bias), resid, flat(gated), d_mixer, buckets)

    seq_bits, batch_bits = index_bits("seq"), index_bits("batch")
    order_a = [seq_bits[0], batch_bits[0], *seq_bits[1:], *batch_bits[1:]]
    order_b = [seq_bits[0], *batch_bits[1:], batch_bits[0], *seq_bits[1:]]
    down_part = scatter_sum(g_down, order_a)
    up_part = scatter_sum(g_up.reshape(hidden_width, width), order_b)

    d_product, g_hidden, g_filter_out, g_decay, g_skip = conv_backward(
        meta, grads, product, spectrum, line(skip_gain), high, back, hidden.astype(bf16), filter_out.astype(bf16),
        line(decay_rate), shaped)
    g_tokens, d_halo, g_in, g_conv, g_conv_bias, g_in_bias, g_norm1_gain, g_norm1_shift = tail(
        meta, mixed, d_product, mixture, cube(d_gated), normed, in_weight, conv_w, conv_b, tokens, halo,
        line(norm1_gain), cube(d_resid))
    arriving = lax.ppermute(d_halo[:, HALO - 2 :], "seq", [(i + 1, i) for i in range(blocks - 1)])
    g_tokens = g_tokens.at[:, rows - 2 :].add(arriving)
    (g_filter_in, g_filter_in_bias, g_filter_mid, g_filter_mid_bias, g_filter_last,
     g_filter_last_bias) = hidden_pull(g_hidden)

    gathered = lax.all_gather(jnp.stack([down_part, up_part]), ("seq", "batch"), axis=0)
    grad_down_weight = unscramble(gathered[:, 0], order_a).astype(f32)
    grad_up = unscramble(gathered[:, 1], order_b).reshape(hidden_width // width, width, width)
    grad_up_weight = grad_up.transpose(1, 0, 2).reshape(width, hidden_width).astype(f32)

    small = [
        g_norm1_gain, g_norm1_shift, g_in_bias, g_conv, g_conv_bias, g_filter_in, g_filter_in_bias,
        g_filter_mid, g_filter_mid_bias, g_filter_last, g_filter_last_bias, g_filter_out, g_decay, g_skip,
        g_out_bias, g_norm2_gain, g_norm2_shift, g_up_bias, g_down_bias,
    ]
    packed = jnp.concatenate([a.reshape(-1) for a in small]).astype(bf16)
    unit = width * 8 * devices
    padded = -(-packed.shape[0] // unit) * unit
    packed = jnp.pad(packed, (0, padded - packed.shape[0])).reshape(-1, width)
    last = jnp.concatenate([g_in.reshape(3 * width, width), g_out, packed], axis=0)
    last = gather_rows(scatter_sum(last, order_a), order_a).astype(f32)
    grad_in_weight = last[: 3 * width].reshape(3, width, width).transpose(1, 0, 2).reshape(width, 3 * width)
    grad_out_weight = last[3 * width : 4 * width]
    flat_small = last[4 * width :].reshape(-1)
    shapes = [
        (width,), (width,), (3 * width,), (3, 3 * width), (3 * width,), filter_in.shape, filter_in_bias.shape,
        filter_mid.shape, filter_mid_bias.shape, filter_last.shape, filter_last_bias.shape, filter_out.shape,
        (width,), (width,), (width,), (width,), (width,), (hidden_width,), (width,),
    ]
    outs, at = [], 0
    for s in shapes:
        size = math.prod(s)
        outs.append(flat_small[at : at + size].reshape(s))
        at += size
    (n1g, n1s, inb, cw, cb, fi, fib, fm, fmb, fl, flb, fo, dr, sg, ob, n2g, n2s, ub, db) = outs
    return (
        cube(block_out), g_tokens, n1g, n1s, grad_in_weight, inb, cw, cb, fi, fib, fm, fmb, fl, flb, fo, dr, sg,
        grad_out_weight, ob, n2g, n2s, grad_up_weight, ub, grad_down_weight, db,
    )


def solution(mesh):
    split = P("batch", "seq", None)
    return jax.shard_map(
        shards,
        mesh=mesh,
        in_specs=(split, split, P("batch")) + (P(),) * 23,
        out_specs=(split, split) + (P(),) * 23,
        check_vma=False,
    )
```

time: 1240 us -> 606 us (0.49)
  matrix products: 438 us -> 17 us
  waiting for transfers between devices: 585 us -> 237 us
  Pallas kernels: 0 us -> 146 us
  other arithmetic: 65.6 us -> 37.9 us
  starting transfers between devices: 4.88 us -> 30.9 us
    psum x2 -> x0, waiting for transfers between devices: 585 us -> none  [shards(): lax.psum((grad_norm1_gain, grad_norm1_shift, grad_in_weight, grad_in_bias...]
    dot_general x39 -> x8, matrix products: 438 us -> 17 us  [the longest x3 8.97 us: filter_hidden(): return jnp.sin(jnp.dot(hidden, filter_last, precision=highest) + last_bias)]
    ppermute x2 -> x28, waiting for transfers between devices: 0.01 us -> 237 us  [the longest x26 234 us: xor_permute(): return lax.ppermute(array, axis, [(i, i ^ bit) for i in range(count)])]
    pallas_call x0 -> x7, Pallas kernels: none -> 146 us  [the longest x1 36.3 us: middle(): pl.pallas_call(partial(middle_body, buckets, rows, steps), grid=(steps,),...]
    rev x2 -> x0, local copies, waits for them, and re-layouts: 49.5 us -> none  [the longest x1 31.7 us: reverse_terms(): jnp.flip(lax.dynamic_slice_in_dim(taps_pad, slice_at, span_len - 1, 0), a...]
    convert_element_type x0 -> x3, local copies, waits for them, and re-layouts: none -> 29.2 us  [the longest x2 24.3 us: shards(): grad_up.transpose(1, 0, 2).reshape(width, hidden_width).astype(f32)]
    ppermute x2 -> x28, starting transfers between devices: 4.5 us -> 30.8 us  [the longest x26 27.2 us: xor_permute(): return lax.ppermute(array, axis, [(i, i ^ bit) for i in range(count)])]
    reduce_sum x9 -> x1, other arithmetic: 20.6 us -> 1.76 us  [filter_hidden(): return jnp.sin(jnp.dot(hidden, filter_last, precision=highest) + last_bias)]
  transfers between devices with their start and end apart: 6 -> 29, of which waited for: 2 -> 17; matrix products, arithmetic and copies ran while one was open for 26% -> 16% of each run, Pallas kernels for 0% -> 11%
where the time goes in v1:
time: 606 us; the launch traced here: 595 us
  waiting for transfers between devices  237 us (39%)
  Pallas kernels  146 us (24%)
  local copies, waits for them, and re-layouts  110 us (18%)
  other arithmetic  37.9 us (6%)
  starting transfers between devices  30.9 us (5%)
  matrix products  17 us (3%)
  between operations  15.5 us (3%)
    ppermute x26, waiting for transfers between devices, xor_permute(): return lax.ppermute(array, axis, [(i, i ^ bit) for i in range(count)])  234 us
    pallas_call x1, Pallas kernels, middle(): pl.pallas_call(partial(middle_body, buckets, rows, steps), grid=(steps,),...  36.3 us
    unnamed x124, local copies, waits for them, and re-layouts  33.5 us
    pallas_call x1, Pallas kernels, tail(): pl.pallas_call(partial(tail_body, buckets, rows, steps), grid=(steps,), i...  31.8 us
    ppermute x26, starting transfers between devices, xor_permute(): return lax.ppermute(array, axis, [(i, i ^ bit) for i in range(count)])  27.2 us
    pallas_call x1, Pallas kernels, weight_grads(): pl.pallas_call(partial(weights_body, buckets, rows, steps), grid=(steps,)...  26 us
    convert_element_type x2, local copies, waits for them, and re-layouts, shards(): grad_up.transpose(1, 0, 2).reshape(width, hidden_width).astype(f32)  24.3 us
    pallas_call x1, Pallas kernels, conv_backward(): pl.pallas_call(partial(conv_back_body, blocks, rows, buckets), grid=(widt...  24.1 us
  transfers between devices with their start and end apart: 29, of which 17 were waited for; matrix products, arithmetic and copies ran while one was open for 16% of the time, Pallas kernels for 11%

profile of v1, /device:TPU:0, one launch (start us, length us, event | category | flops | bytes accessed | tf_op | source)
XLA Modules:
  0.0 594.8 jit_solution(1940037156551136682)
XLA Ops:
  8.2 2.3 collective-permute-start
  16.3 8.8 %front.1 = (bf16[816,768]{1,0:T(8,128)(2,1)S(1)}, bf16[3,3,272,768]{3,2,1,0:T(8,128)(2,1)}, bf16[3,256,768]{2,1,0:T(8,128)(2,1)S(1)}, f32[3,256,768]{2,1,0:T(8,128)S(1)}) custom-call(s32[4]{0:T(128)S(1)} %pad_add_fusion.meta, bf16[3,256,768]{2,1,0:T(8,128)(2,1)S(1)} %copy-done.2, bf16[3,16,768]{2,1,0:T(8,128)(2,1)S(1)} %collective-permute-done.halo, ...), custom_call_target="tpu_custom_call" | custom-call | flops 2887778304 | bytes 16777216 | tf_op jit(solution)/shard_map/front/pallas_call | solution.py:130
  27.6 2.5 collective-permute-start.2
  30.2 25.7 %collective-permute-done.2.refs_2_ = bf16[3,256,768]{2,1,0:T(8,128)(2,1)S(1)} collective-permute-done((bf16[3,256,768]{2,1,0:T(8,128)(2,1)S(1)}, bf16[3,256,768]{2,1,0:T(8,128)(2,1)S(1)}, u32[]{:S(2)}, u32[]{:S(2)}) %collective-permute-start.2) | collective-permute-done | bytes 1179680 | tf_op jit(solution)/shard_map/ppermute | solution.py:28
  59.2 3.2 fusion.8
  62.4 1.9 fusion.9
  64.3 3.4 fusion.10
  69.6 8.9 %filter_spectra.1 = (f32[1024,768]{1,0:T(8,128)S(1)}, f32[4,512,768]{2,1,0:T(8,128)}) custom-call(f32[1024,64]{1,0:T(8,128)S(1)} %get-tuple-element.221.hidden, f32[64,768]{1,0:T(8,128)S(1)} %copy-done.10, f32[1,768]{1,0:T(1,128)S(1)} %reshape.275.decay.refs_11_, bf16[512,256]{1,0:T(8,128)(2,1)S(1)} %copy-done.8, bf16[512,256]{1,0:T(8,128)(2,1)S(1)} %copy-done.19), custom_call_target="tpu_custom_call" | custom-call | flops 4026531840 | bytes 10485760 | tf_op jit(solution)/shard_map/filter_spectra/pallas_call | solution.py:195
  78.5 1.6 copy-done.20
  80.1 10.6 %conv_forward.1 = (f32[3,256,768]{2,1,0:T(8,128)}, bf16[3,256,768]{2,1,0:T(8,128)(2,1)S(1)}) custom-call(s32[4]{0:T(128)S(1)} %copy-done.15, bf16[3,256,768]{2,1,0:T(8,128)(2,1)S(1)} %get-tuple-element.76.refs_0_.refs_4_, bf16[3,256,768]{2,1,0:T(8,128)(2,1)} %collective-permute-done.1.refs_1_, bf16[3,256,768]{2,1,0:T(8,128)(2,1)S(1)} %collective-permute-done.2.refs_2_, ...), custom_call_target="tpu_custom_call" | custom-call | flops 3019898880 | bytes 16777216 | tf_op jit(solution)/shard_map/conv_forward/pallas_call | solution.py:253
  91.8 36.3 %middle.1 = (bf16[768,768]{1,0:T(8,128)(2,1)}, bf16[768,768]{1,0:T(8,128)(2,1)}, f32[768,768]{1,0:T(8,128)}, bf16[768,3072]{1,0:T(8,128)(2,1)}, bf16[768,3072]{1...) custom-call(s32[4]{0:T(128)} %copy-done.14, ...), custom_call_target="tpu_custom_call" | custom-call | flops 10871635968 | bytes 41943040 | tf_op jit(solution)/shard_map/middle/pallas_call | solution.py:355
  128.1 26.0 %weight_grads.1 = (bf16[768,768]{1,0:T(8,128)(2,1)}, bf16[3072,768]{1,0:T(8,128)(2,1)}, bf16[4,768,768]{2,1,0:T(8,128)(2,1)}, bf16[768,768]{1,0:T(8,128)(2,1)}, f32[1,768]{1,0:T(1,128)}) custom-call(s32[4]{0:T(128)} %copy-done.14, bf16[768,3072]{1,0:T(8,128)(2,1)} %get-tuple-element.80.active, bf16[768,3072]{1,0:T(8,128)(2,1)} %get-tuple-element.81.d_up, ...), custom_call_target="tpu_custom_call" | custom-call | flops 10871635968 | bytes 41943040 | tf_op jit(solution)/shard_map/weight_grads/pallas_call | solution.py:420
  154.0 3.4 constant_dynamic-slice_fusion.9
  158.7 1.6 constant_dynamic-slice_fusion.4
  160.3 5.1 collective-permute-start.5
  166.0 26.1 %collective-permute-done.5.refs_2_ = bf16[3,256,768]{2,1,0:T(8,128)(2,1)} collective-permute-done((bf16[3,256,768]{2,1,0:T(8,128)(2,1)S(1)}, bf16[3,256,768]{2,1,0:T(8,128)(2,1)}, u32[]{:S(2)}, u32[]{:S(2)}) %collective-permute-start.5) | collective-permute-done | bytes 1179680 | tf_op jit(solution)/shard_map/ppermute | solution.py:28
  192.1 3.0 add_convert_fusion.2
  197.7 3.0 add_convert_fusion.1
  201.8 1.6 collective-permute-start.24
  204.3 24.1 %conv_backward.1 = (f32[3,256,768]{2,1,0:T(8,128)}, f32[1024,64]{1,0:T(8,128)S(1)}, f32[64,768]{1,0:T(8,128)S(1)}, f32[1,768]{1,0:T(1,128)S(1)}, f32[1,768]{1,0:T(1,128)S(1)}) custom-call(s32[4]{0:T(128)S(1)} %copy-done.16, bf16[3,256,768]{2,1,0:T(8,128)(2,1)S(1)} %bitcast.55, bf16[3,256,768]{2,1,0:T(8,128)(2,1)S(1)} %collective-permute-done.4.refs_1_, ...), custom_call_target="tpu_custom_call" | custom-call | flops 6039797760 | bytes 20971520 | tf_op jit(solution)/shard_map/conv_backward/pallas_call | solution.py:527
  228.4 3.5 fusion.12
  231.9 31.8 %tail.1 = (f32[3,256,768]{2,1,0:T(8,128)}, f32[3,16,768]{2,1,0:T(8,128)}, bf16[3,768,768]{2,1,0:T(8,128)(2,1)}, f32[3,3,768]{2,1,0:T(4,128)}, f32[3,768]{1,0:T(4...) custom-call(s32[4]{0:T(128)} %copy-done.14, bf16[3,3,272,768]{3,2,1,0:T(8,128)(2,1)} %get-tuple-element.87.mixed, ...), custom_call_target="tpu_custom_call" | custom-call | flops 5775556608 | bytes 31457280 | tf_op jit(solution)/shard_map/tail/pallas_call | solution.py:638
  263.7 1.6 add_convert_fusion.5
  265.4 1.6 add_convert_fusion.4
  267.0 2.7 collective-permute-start.25
  269.7 2.1 convolution_convert_fusion
  271.8 6.0 %collective-permute-done.20 = bf16[384,768]{1,0:T(8,128)(2,1)S(1)} collective-permute-done((bf16[384,768]{1,0:T(8,128)(2,1)S(1)}, bf16[384,768]{1,0:T(8,128)(2,1)S(1)}, u32[]{:S(2)}, u32[]{:S(2)}) %collective-permute-start.20) | collective-permute-done | bytes 589856 | tf_op jit(solution)/shard_map/ppermute | solution.py:28
  278.5 14.5 %collective-permute-done.25 = bf16[384,768]{1,0:T(8,128)(2,1)S(1)} collective-permute-done((bf16[384,768]{1,0:T(8,128)(2,1)S(1)}, bf16[384,768]{1,0:T(8,128)(2,1)S(1)}, u32[]{:S(2)}, u32[]{:S(2)}) %collective-permute-start.25) | collective-permute-done | bytes 589856 | tf_op jit(solution)/shard_map/ppermute | solution.py:28
  293.9 2.2 collective-permute-done.21
  296.3 5.9 collective-permute-done.26
  302.4 1.8 collective-permute-start.27
  304.2 3.4 collective-permute-done.27
  309.0 1.6 fusion.11
  311.9 1.8 fusion.3
  315.6 3.2 pad_maximum_fusion
  319.0 2.1 copy-done.23
  321.1 4.9 collective-permute-done.8
  326.0 3.1 add_convert_fusion
  330.9 40.8 %collective-permute-done.9 = bf16[832,768]{1,0:T(8,128)(2,1)} collective-permute-done((bf16[832,768]{1,0:T(8,128)(2,1)}, bf16[832,768]{1,0:T(8,128)(2,1)}, u32[]{:S(2)}, u32[]{:S(2)}) %collective-permute-start.9) | collective-permute-done | bytes 1277984 | tf_op jit(solution)/shard_map/ppermute | solution.py:28
  371.7 1.6 add_convert_fusion.3
  374.4 2.0 collective-permute-start.10
  376.4 21.3 %collective-permute-done.10 = bf16[416,768]{1,0:T(8,128)(2,1)S(1)} collective-permute-done((bf16[416,768]{1,0:T(8,128)(2,1)S(1)}, bf16[416,768]{1,0:T(8,128)(2,1)S(1)}, u32[]{:S(2)}, u32[]{:S(2)}) %collective-permute-start.10) | collective-permute-done | bytes 639008 | tf_op jit(solution)/shard_map/ppermute | solution.py:28
  399.0 1.6 collective-permute-start.11
  400.6 13.4 %collective-permute-done.11 = bf16[208,768]{1,0:T(8,128)(2,1)S(1)} collective-permute-done((bf16[208,768]{1,0:T(8,128)(2,1)S(1)}, bf16[208,768]{1,0:T(8,128)(2,1)S(1)}, u32[]{:S(2)}, u32[]{:S(2)}) %collective-permute-start.11) | collective-permute-done | bytes 319520 | tf_op jit(solution)/shard_map/ppermute | solution.py:28
  414.1 1.7 collective-permute-start.12
  415.8 8.4 %collective-permute-done.12 = bf16[104,768]{1,0:T(8,128)(2,1)S(1)} collective-permute-done((bf16[104,768]{1,0:T(8,128)(2,1)S(1)}, bf16[104,768]{1,0:T(8,128)(2,1)S(1)}, u32[]{:S(2)}, u32[]{:S(2)}) %collective-permute-start.12) | collective-permute-done | bytes 159776 | tf_op jit(solution)/shard_map/ppermute | solution.py:28
  424.4 10.2 %collective-permute-done.13 = bf16[104,768]{1,0:T(8,128)(2,1)S(1)} collective-permute-done((bf16[104,768]{1,0:T(8,128)(2,1)S(1)}, bf16[104,768]{1,0:T(8,128)(2,1)S(1)}, u32[]{:S(2)}, u32[]{:S(2)}) %collective-permute-start.13) | collective-permute-done | bytes 159776 | tf_op jit(solution)/shard_map/ppermute | solution.py:28
  434.7 9.4 %collective-permute-done.14 = bf16[208,768]{1,0:T(8,128)(2,1)S(1)} collective-permute-done((bf16[208,768]{1,0:T(8,128)(2,1)S(1)}, bf16[208,768]{1,0:T(8,128)(2,1)S(1)}, u32[]{:S(2)}, u32[]{:S(2)}) %collective-permute-start.14) | collective-permute-done | bytes 319520 | tf_op jit(solution)/shard_map/ppermute | solution.py:28
  444.4 15.4 %collective-permute-done.15 = bf16[416,768]{1,0:T(8,128)(2,1)S(1)} collective-permute-done((bf16[416,768]{1,0:T(8,128)(2,1)S(1)}, bf16[416,768]{1,0:T(8,128)(2,1)S(1)}, u32[]{:S(2)}, u32[]{:S(2)}) %collective-permute-start.15) | collective-permute-done | bytes 639008 | tf_op jit(solution)/shard_map/ppermute | solution.py:28
  461.2 2.1 collective-permute-start.16
  463.4 26.7 %collective-permute-done.16 = bf16[832,768]{1,0:T(8,128)(2,1)S(1)} collective-permute-done((bf16[832,768]{1,0:T(8,128)(2,1)}, bf16[832,768]{1,0:T(8,128)(2,1)S(1)}, u32[]{:S(2)}, u32[]{:S(2)}) %collective-permute-start.16) | collective-permute-done | bytes 1277984 | tf_op jit(solution)/shard_map/ppermute | solution.py:28
  494.2 2.6 collective-permute-done.7
  496.8 1.5 add_dynamic-update-slice_fusion
  498.3 3.4 broadcast_select_fusion.1
  512.5 2.5 maximum_convert_fusion
  515.0 3.4 slice.157
  518.5 8.3 %copy.69 = f32[768,3,768]{0,2,1:T(8,128)} copy(f32[768,3,768]{2,0,1:T(8,128)} %bitcast.59) | data formatting | bytes 14155776 | tf_op jit(solution)/shard_map/transpose | solution.py:778
  526.7 8.0 %copy.72 = f32[768,2304]{1,0:T(8,128)} copy(f32[768,2304]{0,1:T(8,128)} %bitcast.60) | data formatting | bytes 14155776
  536.5 1.6 maximum_convert_fusion.1
  540.7 6.6 %fusion.4 = (bf16[32,1,96,768]{3,2,1,0:T(8,128)(2,1)}, bf16[32,1,96,768]{3,2,1,0:T(8,128)(2,1)S(1)}) fusion(bf16[32,2,96,768]{3,2,1,0:T(8,128)(2,1)} %bitcast.65), kind=kLoop, calls=%fused_computation.79 | loop fusion | bytes 18874368 | tf_op jit(solution)/shard_map/slice | solution.py:763
  548.5 11.0 %copy.70 = f32[2,2,2,2,2,96,768]{6,1,0,5,4,3,2:T(2,128)} copy(f32[2,2,2,2,2,96,768]{6,5,3,1,2,0,4:T(8,128)S(1)} %convert_bitcast_fusion) | data formatting | bytes 18874368 | tf_op jit(solution)/shard_map/convert_element_type | solution.py:765
  559.5 13.3 %reshape.316 = f32[4,768,768]{2,0,1:T(4,128)} reshape(f32[2,2,2,2,2,96,768]{6,1,0,5,4,3,2:T(2,128)} %copy.70) | data formatting | bytes 18874368 | tf_op jit(solution)/shard_map/convert_element_type | solution.py:765
  572.8 9.8 %copy.74 = f32[96,8,4,768]{3,1,2,0:T(8,128)} copy(f32[96,8,4,768]{3,2,1,0:T(4,128)} %bitcast.58) | data formatting | bytes 18874368
  582.6 4.9 copy.71
  (240 shorter events, 55.2 us)
Async XLA Ops:
  7.2 57.1 %copy-start = (f32[64,64]{1,0:T(8,128)S(1)}, f32[64,64]{1,0:T(8,128)}, u32[]{:S(2)}) copy-start(f32[64,64]{1,0:T(8,128)} %param.45) | copy-start | bytes 49156
  7.2 533.5 %all-gather.3.cloned.1.call-start = ((), (), s32[]{:S(2)}) async-start(), calls=%async_computation | async-start | bytes 9732096 | tf_op jit(solution)/shard_map/all_gather | solution.py:762
  8.2 6.7 %collective-permute-start = (bf16[3,16,768]{2,1,0:T(8,128)(2,1)S(1)}, bf16[3,16,768]{2,1,0:T(8,128)(2,1)S(1)}, u32[]{:S(2)}, u32[]{:S(2)}) collective-permute-start(bf16[3,16,768]{2,1,0:T(8,128)(2,1)S(1)} %slice.125), channel_id=1, source_target_pairs={{0,8},{8,16},{16,24},{1,9},{9,17},{17,25},{2,10},{10,18},{18,26},{... | collective-permute-start | bytes 221192 | tf_op jit(solution)/shard_map/ppermute | solution.py:722
  11.2 13.9 %copy-start.13 = (f32[1,768]{1,0:T(1,128)}, f32[1,768]{1,0:T(1,128)S(1)}, u32[]{:S(2)}) copy-start(f32[1,768]{1,0:T(1,128)S(1)} %reshape.270.gain) | copy-start | bytes 9220
  12.6 12.4 %copy-start.12 = (f32[3,768]{1,0:T(4,128)}, f32[3,768]{1,0:T(4,128)S(1)}, u32[]{:S(2)}) copy-start(f32[3,768]{1,0:T(4,128)S(1)} %reshape.274.cb) | copy-start | bytes 27652
  14.1 10.9 %copy-start.6 = (f32[3,3,768]{2,1,0:T(4,128)}, f32[3,3,768]{2,1,0:T(4,128)S(1)}, u32[]{:S(2)}) copy-start(f32[3,3,768]{2,1,0:T(4,128)S(1)} %reshape.273.cw) | copy-start | bytes 82948
  14.9 10.2 %copy-start.14 = (s32[4]{0:T(128)}, s32[4]{0:T(128)S(1)}, u32[]{:S(2)}) copy-start(s32[4]{0:T(128)S(1)} %pad_add_fusion.meta) | copy-start | bytes 52
  16.2 8.9 %copy-start.7 = (bf16[3,16,768]{2,1,0:T(8,128)(2,1)}, bf16[3,16,768]{2,1,0:T(8,128)(2,1)S(1)}, u32[]{:S(2)}) copy-start(bf16[3,16,768]{2,1,0:T(8,128)(2,1)S(1)} %collective-permute-done.halo) | copy-start | bytes 221188
  16.2 40.6 %copy-start.43 = (f32[768]{0:T(1024)S(1)}, f32[768]{0:T(1024)}, u32[]{:S(2)}) copy-start(f32[768]{0:T(1024)} %param.48) | copy-start | bytes 9220
  16.2 40.6 %copy-start.44 = (f32[768]{0:T(1024)S(1)}, f32[768]{0:T(1024)}, u32[]{:S(2)}) copy-start(f32[768]{0:T(1024)} %param.49) | copy-start | bytes 9220
  16.2 40.6 %copy-start.45 = (f32[768]{0:T(1024)S(1)}, f32[768]{0:T(1024)}, u32[]{:S(2)}) copy-start(f32[768]{0:T(1024)} %param.51) | copy-start | bytes 9220
  16.2 41.2 %copy-start.46 = (f32[768]{0:T(1024)S(1)}, f32[768]{0:T(1024)}, u32[]{:S(2)}) copy-start(f32[768]{0:T(1024)} %param.52) | copy-start | bytes 9220
  16.2 41.8 %copy-start.47 = (f32[768]{0:T(1024)S(1)}, f32[768]{0:T(1024)}, u32[]{:S(2)}) copy-start(f32[768]{0:T(1024)} %param.53) | copy-start | bytes 9220
  16.2 42.4 %copy-start.48 = (f32[768]{0:T(1024)S(1)}, f32[768]{0:T(1024)}, u32[]{:S(2)}) copy-start(f32[768]{0:T(1024)} %param.57) | copy-start | bytes 9220
  16.2 42.9 %copy-start.39 = (f32[33,64]{1,0:T(8,128)S(1)}, f32[33,64]{1,0:T(8,128)}, u32[]{:S(2)}) copy-start(f32[33,64]{1,0:T(8,128)} %param.41) | copy-start | bytes 25348
  16.2 42.9 %copy-start.56 = (f32[64]{0:T(128)S(1)}, f32[64]{0:T(128)}, u32[]{:S(2)}) copy-start(f32[64]{0:T(128)} %param.42) | copy-start | bytes 772
  16.3 46.1 %copy-start.37 = (f32[64,64]{1,0:T(8,128)S(1)}, f32[64,64]{1,0:T(8,128)}, u32[]{:S(2)}) copy-start(f32[64,64]{1,0:T(8,128)} %param.43) | copy-start | bytes 49156
  16.3 46.1 %copy-start.57 = (f32[64]{0:T(128)S(1)}, f32[64]{0:T(128)}, u32[]{:S(2)}) copy-start(f32[64]{0:T(128)} %param.44) | copy-start | bytes 772
  16.3 48.0 %copy-start.55 = (f32[64]{0:T(128)S(1)}, f32[64]{0:T(128)}, u32[]{:S(2)}) copy-start(f32[64]{0:T(128)} %param.46) | copy-start | bytes 772
  27.6 52.5 %copy-start.5 = (bf16[3,256,768]{2,1,0:T(8,128)(2,1)}, bf16[3,256,768]{2,1,0:T(8,128)(2,1)S(1)}, u32[]{:S(2)}) copy-start(bf16[3,256,768]{2,1,0:T(8,128)(2,1)S(1)} %get-tuple-element.76.refs_0_.refs_4_) | copy-start | bytes 3538948
  27.6 40.1 %copy-start.8 = (bf16[512,256]{1,0:T(8,128)(2,1)S(1)}, bf16[512,256]{1,0:T(8,128)(2,1)}, u32[]{:S(2)}) copy-start(bf16[512,256]{1,0:T(8,128)(2,1)} %constant.206.clone.high.refs_7_) | copy-start | bytes 786436
  27.6 28.3 %collective-permute-start.2 = (bf16[3,256,768]{2,1,0:T(8,128)(2,1)S(1)}, bf16[3,256,768]{2,1,0:T(8,128)(2,1)S(1)}, u32[]{:S(2)}, u32[]{:S(2)}) collective-permute-start(bf16[3,256,768]{2,1,0:T(8,128)(2,1)S(1)} %get-tuple-element.76.refs_0_.refs_4_), channel_id=1, source_target_pairs={{0,16},{8,24},{16,0},{24,8},{1,17},{9,25},{17,1},{25,9},{2,18},{10... | collective-permute-start | bytes 3538952 | tf_op jit(solution)/shard_map/ppermute | solution.py:28
  30.1 49.9 %collective-permute-start.1 = (bf16[3,256,768]{2,1,0:T(8,128)(2,1)S(1)}, bf16[3,256,768]{2,1,0:T(8,128)(2,1)}, u32[]{:S(2)}, u32[]{:S(2)}) collective-permute-start(bf16[3,256,768]{2,1,0:T(8,128)(2,1)S(1)} %get-tuple-element.76.refs_0_.refs_4_), channel_id=1, source_target_pairs={{0,8},{8,0},{16,24},{24,16},{1,9},{9,1},{17,25},{25,17},{2,10},{10... | collective-permute-start | bytes 3538952 | tf_op jit(solution)/shard_map/ppermute | solution.py:28
  55.9 24.2 %collective-permute-start.3 = (bf16[3,256,768]{2,1,0:T(8,128)(2,1)S(1)}, bf16[3,256,768]{2,1,0:T(8,128)(2,1)}, u32[]{:S(2)}, u32[]{:S(2)}) collective-permute-start(bf16[3,256,768]{2,1,0:T(8,128)(2,1)S(1)} %collective-permute-done.2.refs_2_), channel_id=1, source_target_pairs={{0,8},{8,0},{16,24},{24,16},{1,9},{9,1},{17,25},{25,17},{2,10},{10... | collective-permute-start | bytes 3538952 | tf_op jit(solution)/shard_map/ppermute | solution.py:28
  69.6 10.5 %copy-start.9 = (bf16[256,512]{1,0:T(8,128)(2,1)S(1)}, bf16[256,512]{1,0:T(8,128)(2,1)}, u32[]{:S(2)}) copy-start(bf16[256,512]{1,0:T(8,128)(2,1)} %constant.208.clone.refs_8_) | copy-start | bytes 786436
  69.6 10.5 %copy-start.15 = (s32[4]{0:T(128)S(1)}, s32[4]{0:T(128)}, u32[]{:S(2)}) copy-start(s32[4]{0:T(128)} %copy-done.14) | copy-start | bytes 52
  157.4 34.7 %collective-permute-start.18 = (bf16[1536,768]{1,0:T(8,128)(2,1)}, bf16[1536,768]{1,0:T(8,128)(2,1)}, u32[]{:S(2)}, u32[]{:S(2)}) collective-permute-start(bf16[1536,768]{1,0:T(8,128)(2,1)} %constant_dynamic-slice_fusion.9), channel_id=1, source_target_pairs={{0,8},{8,0},{16,24},{24,16},{1,9},{9,1},{17,25},{25,17},{2,10},{10... | collective-permute-start | bytes 7077896 | tf_op jit(solution)/shard_map/ppermute | solution.py:28
  158.7 7.2 %copy-start.51 = (f32[1,768]{1,0:T(1,128)S(1)}, f32[1,768]{1,0:T(1,128)}, u32[]{:S(2)}) copy-start(f32[1,768]{1,0:T(1,128)} %get-tuple-element.109) | copy-start | bytes 9220
  158.7 7.2 %copy-start.40 = (f32[1,3072]{1,0:T(1,128)S(1)}, f32[1,3072]{1,0:T(1,128)}, u32[]{:S(2)}) copy-start(f32[1,3072]{1,0:T(1,128)} %get-tuple-element.111) | copy-start | bytes 36868
  160.3 37.4 %collective-permute-start.23 = (bf16[1536,768]{1,0:T(8,128)(2,1)}, bf16[1536,768]{1,0:T(8,128)(2,1)}, u32[]{:S(2)}, u32[]{:S(2)}) collective-permute-start(bf16[1536,768]{1,0:T(8,128)(2,1)} %constant_dynamic-slice_fusion.4), channel_id=1, source_target_pairs={{0,8},{8,0},{16,24},{24,16},{1,9},{9,1},{17,25},{25,17},{2,10},{10... | collective-permute-start | bytes 7077896 | tf_op jit(solution)/shard_map/ppermute | solution.py:28
  160.3 31.8 %collective-permute-start.5 = (bf16[3,256,768]{2,1,0:T(8,128)(2,1)S(1)}, bf16[3,256,768]{2,1,0:T(8,128)(2,1)}, u32[]{:S(2)}, u32[]{:S(2)}) collective-permute-start(bf16[3,256,768]{2,1,0:T(8,128)(2,1)S(1)} %bitcast.53), channel_id=1, source_target_pairs={{0,16},{8,24},{16,0},{24,8},{1,17},{9,25},{17,1},{25,9},{2,18},{10... | collective-permute-start | bytes 3538952 | tf_op jit(solution)/shard_map/ppermute | solution.py:28
  165.6 37.8 %collective-permute-start.4 = (bf16[3,256,768]{2,1,0:T(8,128)(2,1)S(1)}, bf16[3,256,768]{2,1,0:T(8,128)(2,1)S(1)}, u32[]{:S(2)}, u32[]{:S(2)}) collective-permute-start(bf16[3,256,768]{2,1,0:T(8,128)(2,1)S(1)} %bitcast.54), channel_id=1, source_target_pairs={{0,8},{8,0},{16,24},{24,16},{1,9},{9,1},{17,25},{25,17},{2,10},{10... | collective-permute-start | bytes 3538952 | tf_op jit(solution)/shard_map/ppermute | solution.py:28
  192.1 11.2 %collective-permute-start.6 = (bf16[3,256,768]{2,1,0:T(8,128)(2,1)}, bf16[3,256,768]{2,1,0:T(8,128)(2,1)S(1)}, u32[]{:S(2)}, u32[]{:S(2)}) collective-permute-start(bf16[3,256,768]{2,1,0:T(8,128)(2,1)} %collective-permute-done.5.refs_2_), channel_id=1, source_target_pairs={{0,8},{8,0},{16,24},{24,16},{1,9},{9,1},{17,25},{25,17},{2,10},{10... | collective-permute-start | bytes 3538952 | tf_op jit(solution)/shard_map/ppermute | solution.py:28
  196.2 67.5 %collective-permute-start.19 = (bf16[768,768]{1,0:T(8,128)(2,1)}, bf16[768,768]{1,0:T(8,128)(2,1)}, u32[]{:S(2)}, u32[]{:S(2)}) collective-permute-start(bf16[768,768]{1,0:T(8,128)(2,1)} %constant_dynamic-slice_fusion.8), channel_id=1, source_target_pairs={{0,1},{1,0},{2,3},{3,2},{4,5},{5,4},{6,7},{7,6},{8,9},{9,8},{10,11... | collective-permute-start | bytes 3538952 | tf_op jit(solution)/shard_map/ppermute | solution.py:28
  201.8 63.6 %collective-permute-start.24 = (bf16[768,768]{1,0:T(8,128)(2,1)}, bf16[768,768]{1,0:T(8,128)(2,1)}, u32[]{:S(2)}, u32[]{:S(2)}) collective-permute-start(bf16[768,768]{1,0:T(8,128)(2,1)} %constant_dynamic-slice_fusion.3), channel_id=1, source_target_pairs={{0,2},{1,3},{2,0},{3,1},{4,6},{5,7},{6,4},{7,5},{8,10},{9,11},{10,... | collective-permute-start | bytes 3538952 | tf_op jit(solution)/shard_map/ppermute | solution.py:28
  204.3 24.1 %copy-start.26 = (f32[1024,64]{1,0:T(8,128)S(1)}, f32[1024,64]{1,0:T(8,128)}, u32[]{:S(2)}) copy-start(f32[1024,64]{1,0:T(8,128)} %get-tuple-element.222) | copy-start | bytes 786436
  204.3 24.1 %copy-start.36 = (f32[1024,64]{0,1:T(8,128)S(1)}, f32[1024,64]{0,1:T(8,128)}, u32[]{:S(2)}) copy-start(f32[1024,64]{0,1:T(8,128)} %get-tuple-element.220) | copy-start | bytes 786436
  265.3 12.5 %collective-permute-start.20 = (bf16[384,768]{1,0:T(8,128)(2,1)S(1)}, bf16[384,768]{1,0:T(8,128)(2,1)S(1)}, u32[]{:S(2)}, u32[]{:S(2)}) collective-permute-start(bf16[384,768]{1,0:T(8,128)(2,1)S(1)} %constant_dynamic-slice_fusion.7), channel_id=1, source_target_pairs={{0,16},{8,24},{16,0},{24,8},{1,17},{9,25},{17,1},{25,9},{2,18},{10... | collective-permute-start | bytes 1769480 | tf_op jit(solution)/shard_map/ppermute | solution.py:28
  267.0 26.0 %collective-permute-start.25 = (bf16[384,768]{1,0:T(8,128)(2,1)S(1)}, bf16[384,768]{1,0:T(8,128)(2,1)S(1)}, u32[]{:S(2)}, u32[]{:S(2)}) collective-permute-start(bf16[384,768]{1,0:T(8,128)(2,1)S(1)} %constant_dynamic-slice_fusion.2), channel_id=1, source_target_pairs={{0,4},{1,5},{2,6},{3,7},{4,0},{5,1},{6,2},{7,3},{8,12},{9,13},{10,... | collective-permute-start | bytes 1769480 | tf_op jit(solution)/shard_map/ppermute | solution.py:28
  278.0 18.1 %collective-permute-start.21 = (bf16[192,768]{1,0:T(8,128)(2,1)S(1)}, bf16[192,768]{1,0:T(8,128)(2,1)S(1)}, u32[]{:S(2)}, u32[]{:S(2)}) collective-permute-start(bf16[192,768]{1,0:T(8,128)(2,1)S(1)} %constant_dynamic-slice_fusion.6), channel_id=1, source_target_pairs={{0,2},{1,3},{2,0},{3,1},{4,6},{5,7},{6,4},{7,5},{8,10},{9,11},{10,... | collective-permute-start | bytes 884744 | tf_op jit(solution)/shard_map/ppermute | solution.py:28
  293.2 15.2 %copy-start.32 = (f32[1024,64]{0,1:T(8,128)S(1)}, f32[1024,64]{0,1:T(8,128)}, u32[]{:S(2)}) copy-start(f32[1024,64]{0,1:T(8,128)} %copy-done.31) | copy-start | bytes 786436
  293.3 15.7 %copy-start.42 = (f32[3,768]{1,0:T(4,128)S(1)}, f32[3,768]{1,0:T(4,128)}, u32[]{:S(2)}) copy-start(f32[3,768]{1,0:T(4,128)} %get-tuple-element.101) | copy-start | bytes 27652
  293.3 15.7 %copy-start.41 = (f32[3,768]{1,0:T(4,128)S(1)}, f32[3,768]{1,0:T(4,128)}, u32[]{:S(2)}) copy-start(f32[3,768]{1,0:T(4,128)} %get-tuple-element.103) | copy-start | bytes 27652
  293.3 15.8 %copy-start.35 = (f32[1024,64]{0,1:T(8,128)S(1)}, f32[1024,64]{0,1:T(8,128)}, u32[]{:S(2)}) copy-start(f32[1024,64]{0,1:T(8,128)} %get-tuple-element.218) | copy-start | bytes 786436
  293.3 8.9 %collective-permute-start.26 = (bf16[192,768]{1,0:T(8,128)(2,1)S(1)}, bf16[192,768]{1,0:T(8,128)(2,1)S(1)}, u32[]{:S(2)}, u32[]{:S(2)}) collective-permute-start(bf16[192,768]{1,0:T(8,128)(2,1)S(1)} %constant_dynamic-slice_fusion.1), channel_id=1, source_target_pairs={{0,1},{1,0},{2,3},{3,2},{4,5},{5,4},{6,7},{7,6},{8,9},{9,8},{10,11... | collective-permute-start | bytes 884744 | tf_op jit(solution)/shard_map/ppermute | solution.py:28
  296.2 14.4 %copy-start.33 = (f32[1024,33]{1,0:T(8,128)S(1)}, f32[1024,33]{1,0:T(8,128)}, u32[]{:S(2)}) copy-start(f32[1024,33]{1,0:T(8,128)} %constant.209.clone) | copy-start | bytes 405508
  296.2 7.9 %collective-permute-start.22 = (bf16[96,768]{1,0:T(8,128)(2,1)S(1)}, bf16[96,768]{1,0:T(8,128)(2,1)S(1)}, u32[]{:S(2)}, u32[]{:S(2)}) collective-permute-start(bf16[96,768]{1,0:T(8,128)(2,1)S(1)} %constant_dynamic-slice_fusion.5), channel_id=1, source_target_pairs={{0,4},{1,5},{2,6},{3,7},{4,0},{5,1},{6,2},{7,3},{8,12},{9,13},{10,... | collective-permute-start | bytes 442376 | tf_op jit(solution)/shard_map/ppermute | solution.py:28
  302.3 9.4 %copy-start.38 = (f32[3,3,768]{2,1,0:T(4,128)S(1)}, f32[3,3,768]{2,1,0:T(4,128)}, u32[]{:S(2)}) copy-start(f32[3,3,768]{2,1,0:T(4,128)} %get-tuple-element.102) | copy-start | bytes 82948
  302.3 9.5 %copy-start.53 = (f32[1,768]{1,0:T(1,128)S(1)}, f32[1,768]{1,0:T(1,128)}, u32[]{:S(2)}) copy-start(f32[1,768]{1,0:T(1,128)} %get-tuple-element.99) | copy-start | bytes 9220
  302.4 9.5 %copy-start.54 = (f32[1,768]{1,0:T(1,128)S(1)}, f32[1,768]{1,0:T(1,128)}, u32[]{:S(2)}) copy-start(f32[1,768]{1,0:T(1,128)} %get-tuple-element.100) | copy-start | bytes 9220
  302.4 5.2 collective-permute-start.27
  321.1 4.9 collective-permute-start.8
  330.3 41.4 %collective-permute-start.9 = (bf16[832,768]{1,0:T(8,128)(2,1)}, bf16[832,768]{1,0:T(8,128)(2,1)}, u32[]{:S(2)}, u32[]{:S(2)}) collective-permute-start(bf16[832,768]{1,0:T(8,128)(2,1)} %constant_dynamic-slice_fusion.13), channel_id=1, source_target_pairs={{0,1},{1,0},{2,3},{3,2},{4,5},{5,4},{6,7},{7,6},{8,9},{9,8},{10,11... | collective-permute-start | bytes 3833864 | tf_op jit(solution)/shard_map/ppermute | solution.py:28
  374.4 23.3 %collective-permute-start.10 = (bf16[416,768]{1,0:T(8,128)(2,1)S(1)}, bf16[416,768]{1,0:T(8,128)(2,1)S(1)}, u32[]{:S(2)}, u32[]{:S(2)}) collective-permute-start(bf16[416,768]{1,0:T(8,128)(2,1)S(1)} %constant_dynamic-slice_fusion.12), channel_id=1, source_target_pairs={{0,16},{8,24},{16,0},{24,8},{1,17},{9,25},{17,1},{25,9},{2,18},{10... | collective-permute-start | bytes 1916936 | tf_op jit(solution)/shard_map/ppermute | solution.py:28
  399.0 14.9 %collective-permute-start.11 = (bf16[208,768]{1,0:T(8,128)(2,1)S(1)}, bf16[208,768]{1,0:T(8,128)(2,1)S(1)}, u32[]{:S(2)}, u32[]{:S(2)}) collective-permute-start(bf16[208,768]{1,0:T(8,128)(2,1)S(1)} %constant_dynamic-slice_fusion.11), channel_id=1, source_target_pairs={{0,2},{1,3},{2,0},{3,1},{4,6},{5,7},{6,4},{7,5},{8,10},{9,11},{10,... | collective-permute-start | bytes 958472 | tf_op jit(solution)/shard_map/ppermute | solution.py:28
  414.1 10.2 %collective-permute-start.12 = (bf16[104,768]{1,0:T(8,128)(2,1)S(1)}, bf16[104,768]{1,0:T(8,128)(2,1)S(1)}, u32[]{:S(2)}, u32[]{:S(2)}) collective-permute-start(bf16[104,768]{1,0:T(8,128)(2,1)S(1)} %constant_dynamic-slice_fusion.10), channel_id=1, source_target_pairs={{0,4},{1,5},{2,6},{3,7},{4,0},{5,1},{6,2},{7,3},{8,12},{9,13},{10,... | collective-permute-start | bytes 479240 | tf_op jit(solution)/shard_map/ppermute | solution.py:28
  424.3 10.3 %collective-permute-start.13 = (bf16[104,768]{1,0:T(8,128)(2,1)S(1)}, bf16[104,768]{1,0:T(8,128)(2,1)S(1)}, u32[]{:S(2)}, u32[]{:S(2)}) collective-permute-start(bf16[104,768]{1,0:T(8,128)(2,1)S(1)} %add_convert_fusion.12), channel_id=1, source_target_pairs={{0,4},{1,5},{2,6},{3,7},{4,0},{5,1},{6,2},{7,3},{8,12},{9,13},{10,... | collective-permute-start | bytes 479240 | tf_op jit(solution)/shard_map/ppermute | solution.py:28
  434.6 9.5 %collective-permute-start.14 = (bf16[208,768]{1,0:T(8,128)(2,1)S(1)}, bf16[208,768]{1,0:T(8,128)(2,1)S(1)}, u32[]{:S(2)}, u32[]{:S(2)}) collective-permute-start(bf16[208,768]{1,0:T(8,128)(2,1)S(1)} %pad_maximum_fusion.4), channel_id=1, source_target_pairs={{0,2},{1,3},{2,0},{3,1},{4,6},{5,7},{6,4},{7,5},{8,10},{9,11},{10,... | collective-permute-start | bytes 958472 | tf_op jit(solution)/shard_map/ppermute | solution.py:28
  444.3 15.5 %collective-permute-start.15 = (bf16[416,768]{1,0:T(8,128)(2,1)S(1)}, bf16[416,768]{1,0:T(8,128)(2,1)S(1)}, u32[]{:S(2)}, u32[]{:S(2)}) collective-permute-start(bf16[416,768]{1,0:T(8,128)(2,1)S(1)} %pad_maximum_fusion.3), channel_id=1, source_target_pairs={{0,16},{8,24},{16,0},{24,8},{1,17},{9,25},{17,1},{25,9},{2,18},{10... | collective-permute-start | bytes 1916936 | tf_op jit(solution)/shard_map/ppermute | solution.py:28
  461.2 28.8 %collective-permute-start.16 = (bf16[832,768]{1,0:T(8,128)(2,1)}, bf16[832,768]{1,0:T(8,128)(2,1)S(1)}, u32[]{:S(2)}, u32[]{:S(2)}) collective-permute-start(bf16[832,768]{1,0:T(8,128)(2,1)} %pad_maximum_fusion.2), channel_id=1, source_target_pairs={{0,1},{1,0},{2,3},{3,2},{4,5},{5,4},{6,7},{7,6},{8,9},{9,8},{10,11... | collective-permute-start | bytes 3833864 | tf_op jit(solution)/shard_map/ppermute | solution.py:28
  492.0 6.3 %collective-permute-start.17 = (bf16[1664,768]{1,0:T(8,128)(2,1)S(1)}, bf16[1664,768]{1,0:T(8,128)(2,1)}, u32[]{:S(2)}, u32[]{:S(2)}) collective-permute-start(bf16[1664,768]{1,0:T(8,128)(2,1)S(1)} %pad_maximum_fusion.1), channel_id=1, source_target_pairs={{0,8},{8,0},{16,24},{24,16},{1,9},{9,1},{17,25},{25,17},{2,10},{10... | collective-permute-start | bytes 7667720 | tf_op jit(solution)/shard_map/ppermute | solution.py:28
  492.9 3.9 collective-permute-start.7
  572.8 9.8 %slice-start = ((s8[4718592]{0:T(1024)(128)(4,1)}), s8[4194304]{0:T(1024)(128)(4,1)S(1)}, s32[]{:S(2)}) async-start(s8[4718592]{0:T(1024)(128)(4,1)} %bitcast.61), calls=%async_computation.1 | async-start | bytes 8388608
  572.8 9.8 %slice-start.1 = ((s8[4718592]{0:T(1024)(128)(4,1)}), s8[524288]{0:T(1024)(128)(4,1)S(1)}, s32[]{:S(2)}) async-start(s8[4718592]{0:T(1024)(128)(4,1)} %bitcast.61), calls=%async_computation.2 | async-start | bytes 1048576
  (27 other events, 74.3 us)
Sparse Core Ops, SparseCore 0:
  308.5 104.0 all-gather.2
